TPU v7x, 128 devices: a whole 4x4x4 slice. The times are simulated.
128 devices in a mesh: wide: 16 (over x, z), narrow: 8 (over y, core).
Axes of the slice: x: 4, y: 4, z: 4, core: 2. Of those that a mesh axis runs over, the one named last changes fastest.
Arguments:
- fine_nodes: float32 [262144, 128], P(('wide', 'narrow')), may hold values from -6 to 6
- fine_edges: float32 [1048576, 128], P(('wide', 'narrow')), may hold values from -6 to 6
- fine_sender: int32 [1048576], P(('wide', 'narrow')), may hold values from 0 to 2815, as said below
- fine_offset: int32 [1048576], P(('wide', 'narrow')), may hold values from 0 to 128, as said below
- fine_send: int32 [128, 8, 96], P(('wide', 'narrow')), may hold values from 0 to 2047
- coarse_edges: float32 [65536, 128], P('wide'), may hold values from -6 to 6
- coarse_sender: int32 [65536], P('wide'), may hold values from 0 to 1279, as said below
- coarse_offset: int32 [65536], P('wide'), may hold values from 0 to 128, as said below
- coarse_send: int32 [16, 4, 64], P('wide'), may hold values from 0 to 1023
- restrict_source: int32 [655360], P(('wide', 'narrow')), may hold values from 0 to 2047
- restrict_offset: int32 [655360], P(('wide', 'narrow')), may hold values from 0 to 128
- restrict_tile: int32 [5120], P(('wide', 'narrow')), may hold values from 0 to 7
- restrict_weight: int32 [655360], P(('wide', 'narrow')), may hold values from 0 to 15
- prolong_index: int32 [3, 262144], P(None, ('wide', 'narrow')), may hold values from 0 to 1023
- prolong_weight: int32 [3, 262144], P(None, ('wide', 'narrow')), may hold values from 0 to 15
- restrict_table: float32 [16], replicated, may hold values from 0.2 to 2
- prolong_table: float32 [16], replicated, may hold values from 0.2 to 2
- edge_w1: float32 [4, 384, 128], replicated, may hold values from -0.3125 to 0.3125
- edge_w2: float32 [4, 128, 128], replicated, may hold values from -0.5 to 0.5
- node_w1: float32 [4, 256, 128], replicated, may hold values from -0.375 to 0.375
- node_w2: float32 [4, 128, 128], replicated, may hold values from -0.5 to 0.5
Outputs:
- fine_out: float32 [262144, 128], P(('wide', 'narrow'))
- coarse_out: float32 [16384, 128], P('wide')
Inputs may be any that keep to these rules, and one draw needn't show every extreme that they name: `fine_sender`: values below 2048 name the device's own nodes; value 2048 + k * 96 + j names the j-th row that the neighbour of offset k sends to it; every such row is named by some slot whose offset is below 128. `fine_offset`: the value 128 marks an empty slot. `coarse_sender`: values below 1024 name the owner's own coarse nodes; value 1024 + k * 64 + j names the j-th row that the neighbour of offset k sends to it; every such row is named by some slot whose offset is below 128. `coarse_offset`: the value 128 marks an empty slot. fine_send[s, k, j] is the node of device s (local index) sent as the j-th row to the device at offset k from s. coarse_send[s, k, j] is the coarse node of owner s (local index) sent as the j-th row to the owner at offset k from s. `restrict_source`: local index of a node of the device. `restrict_offset`: the value 128 marks an empty entry. `restrict_tile`: tile among the coarse nodes of the device's wide owner. `prolong_index`: local index among the coarse nodes of the fine node's wide owner.
All inputs are finite; a program needn't handle non-finite values.
Results may differ from a plain program's by a relative error of at most 0.0003.
Values sent between devices are 32-bit elements; how exact they have to be, the bound alone decides.
A program may use at most 128 MiB of HBM per device.

v0:
```python
import jax
import jax.numpy as jnp
from jax import lax
from jax.sharding import PartitionSpec as P

TILE = 128
RATIO = 16


highest = lax.Precision.HIGHEST


def from_behind(block, axis, distance):
    devices = range(lax.axis_size(axis))
    route = [(i - distance, i) for i in devices if i - distance in devices]
    return lax.ppermute(block, axis, route)


def matmul(operand, weights):
    return jnp.dot(operand, weights, precision=highest, preferred_element_type=jnp.float32)


def layer_norm(values):
    center = values - jnp.mean(values, axis=-1, keepdims=True)
    spread = jnp.mean(center * center, axis=-1, keepdims=True)
    return center * lax.rsqrt(spread + 1e-05)


def lookup(level_index, weight_table):
    levels = jnp.arange(weight_table.shape[0], dtype=jnp.int32)
    return jnp.sum((level_index[..., None] == levels).astype(jnp.float32) * weight_table, axis=-1)


def graph_step(
    receivers, source_rows, edge_rows, sender, offset, edge_in, edge_out, node_in, node_out
):
    latent = receivers.shape[1]
    tile_count = receivers.shape[0] // TILE
    per_tile = edge_rows.shape[0] // tile_count
    target = jnp.arange(edge_rows.shape[0], dtype=jnp.int32) // per_tile * TILE + jnp.minimum(
        offset, TILE - 1
    )
    hidden = matmul(edge_rows, edge_in[:latent]) + matmul(
        source_rows[sender], edge_in[latent : 2 * latent]
    )
    hidden = hidden + matmul(receivers[target], edge_in[2 * latent :])
    new_edges = edge_rows + layer_norm(matmul(jax.nn.relu(hidden), edge_out))
    onehot = (
        offset.reshape(tile_count, per_tile)[:, :, None] == jnp.arange(TILE, dtype=jnp.int32)
    ).astype(jnp.float32)
    summed = jnp.einsum(
        "tej,teh->tjh", onehot, new_edges.reshape(tile_count, per_tile, latent), precision=highest
    )
    summed = summed.reshape(-1, latent)
    node_hidden = matmul(receivers, node_in[:latent]) + matmul(summed, node_in[latent:])
    return (receivers + layer_norm(matmul(jax.nn.relu(node_hidden), node_out)), new_edges)


def restrict_partial(fine_rows, source, offset, tile_id, weight_index, weight_table, tile_count):
    blocks = tile_id.shape[0]
    latent = fine_rows.shape[1]
    picked = fine_rows[source].reshape(blocks, TILE, latent)
    scales = lookup(weight_index, weight_table).reshape(blocks, TILE)
    onehot = (offset.reshape(blocks, TILE)[:, :, None] == jnp.arange(TILE, dtype=jnp.int32)).astype(
        jnp.float32
    )
    onehot = onehot * scales[:, :, None]
    contrib = jnp.einsum("bej,beh->bjh", onehot, picked, precision=highest)
    weight_sum = jnp.sum(onehot, axis=1)
    select = (tile_id[:, None] == jnp.arange(tile_count, dtype=jnp.int32)).astype(jnp.float32)
    numer = jnp.einsum("bt,bjh->tjh", select, contrib, precision=highest).reshape(-1, latent)
    denom = jnp.einsum("bt,bj->tj", select, weight_sum, precision=highest).reshape(-1)
    return (numer, denom)


def prolong_rows(owner_rows, index_rows, weight_index, weight_table):
    scales = lookup(weight_index, weight_table)
    picked = owner_rows[index_rows]
    return jnp.sum(scales[:, :, None] * picked, axis=0) / jnp.sum(scales, axis=0)[:, None]


def local(
    fine_nodes,
    fine_edges,
    fine_sender,
    fine_offset,
    fine_send,
    coarse_edges,
    coarse_sender,
    coarse_offset,
    coarse_send,
    restrict_source,
    restrict_offset,
    restrict_tile,
    restrict_weight,
    prolong_index,
    prolong_weight,
    restrict_table,
    prolong_table,
    edge_w1,
    edge_w2,
    node_w1,
    node_w2,
):
    latent = fine_nodes.shape[1]
    narrow_count = lax.axis_size("narrow")

    def fine_neighbours(node_rows):
        outgoing = node_rows[fine_send[0]]
        along = []
        for side, picks in ((-1, (0, 3, 5)), (1, (2, 4, 7))):
            bundle = jnp.stack([outgoing[picks[0]], outgoing[picks[1]], outgoing[picks[2]]], axis=0)
            along.append(from_behind(bundle, "narrow", side))
        across = []
        for side, place, own_pick in ((-1, 0, 1), (1, 2, 6)):
            bundle = jnp.stack([along[0][place], outgoing[own_pick], along[1][place]], axis=0)
            across.append(from_behind(bundle, "wide", side))
        halo_rows = jnp.concatenate([across[0], along[0][1:2], along[1][1:2], across[1]], axis=0)
        return halo_rows.reshape(-1, latent)

    def fine_step(node_rows, edge_rows, section_index):
        extended = jnp.concatenate([node_rows, fine_neighbours(node_rows)], axis=0)
        return graph_step(
            node_rows,
            extended,
            edge_rows,
            fine_sender,
            fine_offset,
            edge_w1[section_index],
            edge_w2[section_index],
            node_w1[section_index],
            node_w2[section_index],
        )

    first_nodes, first_edges = fine_step(fine_nodes, fine_edges, 0)
    tile_count = first_nodes.shape[0] * narrow_count // RATIO // TILE
    numer, denom = restrict_partial(
        first_nodes,
        restrict_source,
        restrict_offset,
        restrict_tile,
        restrict_weight,
        restrict_table,
        tile_count,
    )
    numer, denom = (
        lax.psum_scatter(numer, "narrow", scatter_dimension=0, tiled=True),
        lax.psum_scatter(denom, "narrow", scatter_dimension=0, tiled=True),
    )
    own_rows = numer / (1.0 + denom)[:, None]

    def gather_rows(share_rows):
        return lax.all_gather(share_rows, "narrow", axis=0, tiled=True)

    per_edges = coarse_edges.shape[0] // narrow_count
    start_slot = lax.axis_index("narrow") * per_edges
    edge_own = lax.dynamic_slice_in_dim(coarse_edges, start_slot, per_edges, 0)
    sender_own = lax.dynamic_slice_in_dim(coarse_sender, start_slot, per_edges, 0)
    offset_own = lax.dynamic_slice_in_dim(coarse_offset, start_slot, per_edges, 0)
    for section_index in (1, 2):
        coarse_coarse_full = gather_rows(own_rows)
        coarse_outgoing = coarse_coarse_full[coarse_send[0]]
        pieces = []
        for index, coarse_side in enumerate((-2, -1, 1, 2)):
            pieces.append(from_behind(coarse_outgoing[index], "wide", coarse_side))
        extended = jnp.concatenate([coarse_coarse_full] + pieces, axis=0)
        own_rows, edge_own = graph_step(
            own_rows,
            extended,
            edge_own,
            sender_own,
            offset_own,
            edge_w1[section_index],
            edge_w2[section_index],
            node_w1[section_index],
            node_w2[section_index],
        )
    coarse_full = gather_rows(own_rows)
    prolonged = prolong_rows(coarse_full, prolong_index, prolong_weight, prolong_table)
    final_nodes, final_edges = fine_step(first_nodes + prolonged, first_edges, 3)
    return (final_nodes, coarse_full)


def solution(mesh):
    placed = (
        P(("wide", "narrow"), None),
        P(("wide", "narrow"), None),
        P(("wide", "narrow")),
        P(("wide", "narrow")),
        P(("wide", "narrow"), None, None),
        P("wide", None),
        P("wide"),
        P("wide"),
        P("wide", None, None),
        P(("wide", "narrow")),
        P(("wide", "narrow")),
        P(("wide", "narrow")),
        P(("wide", "narrow")),
        P(None, ("wide", "narrow")),
        P(None, ("wide", "narrow")),
        P(),
        P(),
        P(),
        P(),
        P(),
        P(),
    )
    return jax.shard_map(
        local,
        mesh=mesh,
        in_specs=placed,
        out_specs=(P(("wide", "narrow"), None), P("wide", None)),
        check_vma=False,
    )
```

profile of v0, /device:TPU:14, one launch (start us, length us, event | category | flops | bytes accessed | tf_op | source)
XLA Modules:
  0.0 461.7 jit_solution(11018207344915507239)
XLA Ops:
  24.5 6.6 %fusion.71 = f32[8192,128]{1,0:T(8,128)} fusion(f32[8192,128]{1,0:T(8,128)} %param.22, f32[4,384,128]{2,1,0:T(8,128)} %param.38), kind=kOutput, calls=%fused_computation.133 | convolution fusion | flops 1610612736 | bytes 8454144 | tf_op jit(solution)/shard_map/dot_general | solution.py:20
  35.5 6.2 %collective-permute-start.2 = (f32[3,96,128]{2,1,0:T(8,128)}, f32[3,96,128]{2,1,0:T(8,128)}, u32[]{:S(2)}, u32[]{:S(2)}) collective-permute-start(f32[3,96,128]{2,1,0:T(8,128)} %pad_maximum_fusion.6), channel_id=1, source_target_pairs={{8,0},{16,8},{24,16},{32,24},{40,32},{48,40},{56,48},{64,56},{72,6... | collective-permute-start | bytes 442376 | tf_op jit(solution)/shard_map/ppermute | solution.py:16
  47.1 27.9 %gather_fusion.2 = f32[8192,128]{1,0:T(8,128)} fusion(f32[2048,128]{1,0:T(8,128)S(1)} %copy-done.2, s32[8192]{0:T(1024)S(1)} %fusion.108), kind=kCustom, calls=%fused_computation.2 | custom fusion | bytes 8421376 | tf_op jit(solution)/shard_map/gather | solution.py:46
  76.3 12.5 %all-reduce = f32[1024]{0:T(1024)} all-reduce(f32[1024]{0:T(1024)S(1)} %convolution_bitcast_fusion), channel_id=3, replica_groups=mesh['wide'=16,'narrow'=8] {'narrow'}, use_global_device_ids=true, to_apply=%region_8.9.clone | all-reduce | flops 1024 | bytes 8192
  90.0 27.9 %gather_fusion.1 = f32[8192,128]{1,0:T(8,128)} fusion(f32[2816,128]{1,0:T(8,128)S(1)} %pad_maximum_fusion, s32[8192]{0:T(1024)S(1)} %fusion.107), kind=kCustom, calls=%fused_computation.1 | custom fusion | bytes 8421376 | tf_op jit(solution)/shard_map/gather | solution.py:44
  117.8 6.3 %convolution_add_fusion.3 = f32[8192,128]{1,0:T(8,128)S(1)} fusion(f32[8192,128]{1,0:T(8,128)} %fusion.71, f32[8192,128]{1,0:T(8,128)} %gather_fusion.1, f32[4,384,128]{2,1,0:T(8,128)} %param.38), kind=kOutput, calls=%fused_computation.19 | convolution fusion | flops 1611661312 | bytes 12648448 | tf_op jit(solution)/shard_map/dot_general | solution.py:20
  124.1 4.4 fusion.1
  128.5 4.4 fusion.127
  135.5 4.9 %multiply_add_fusion.1 = f32[8192,128]{1,0:T(8,128)S(1)} fusion(f32[8192,128]{1,0:T(8,128)S(1)} %copy-done.6, f32[8192,128]{1,0:T(8,128)S(1)} %get-tuple-element.51, f32[8192]{0:T(1024)S(1)} %add_rsqrt_fusion.1, f32[8192]{0:T(1024)S(1)} %broadcast_multiply_fusion.1), kind=kLoop, calls=%fused_computation.22 | loop fusion | flops 3145728 | bytes 12648448 | tf_op jit(solution)/shard_map/add | solution.py:47
  147.8 17.8 %gather_fusion.3 = f32[5120,128]{1,0:T(8,128)} fusion(f32[2048,128]{1,0:T(8,128)S(1)} %copy.102, s32[5120]{0:T(1024)S(1)} %copy-done.27), kind=kCustom, calls=%fused_computation.3 | custom fusion | bytes 5263360 | tf_op jit(solution)/shard_map/gather | solution.py:62
  165.6 4.9 %fusion.4 = f32[40,128,128]{2,1,0:T(8,128)S(1)} fusion(f32[40,128,128]{2,1,0:T(8,128)} %bitcast.193, f32[40,128]{1,0:T(8,128)S(1)} %bitcast.200, s32[40,128]{1,0:T(8,128)S(1)} %bitcast.202), kind=kOutput, calls=%fused_computation.28 | convolution fusion | flops 1007943680 | bytes 5283840 | tf_op jit(solution)/shard_map/bej,beh->bjh/dot_general | solution.py:68
  179.8 24.5 %reduce-scatter.2.cloned.1.call-done = f32[128,128]{0,1:T(8,128)} async-done(((f32[1024,128]{0,1:T(8,128)}), f32[128,128]{0,1:T(8,128)}) %reduce-scatter.2.cloned.1.call-update) | async-done | bytes 65552 | tf_op jit(solution)/shard_map/reduce_scatter | solution.py:147
  205.2 13.6 %all_gather.9 = f32[1024,128]{0,1:T(8,128)S(1)} all-gather(f32[128,128]{0,1:T(8,128)S(1)} %broadcast_divide_fusion), channel_id=1, replica_groups=mesh['wide'=16,'narrow'=8] {'narrow'}, dimensions={0}, use_global_device_ids=true | all-gather | bytes 589824 | tf_op jit(solution)/shard_map/all_gather | solution.py:153
  219.9 5.4 %collective-permute-start.4 = (f32[64,128]{0,1:T(8,128)S(1)}, f32[64,128]{0,1:T(8,128)S(1)}, u32[]{:S(2)}, u32[]{:S(2)}) collective-permute-start(f32[64,128]{0,1:T(8,128)S(1)} %copy.130), channel_id=1, source_target_pairs={{16,0},{24,8},{32,16},{40,24},{48,32},{56,40},{64,48},{72,56},{80,... | collective-permute-start | bytes 98312 | tf_op jit(solution)/shard_map/ppermute | solution.py:16
  236.9 3.0 collective-permute-done.7
  249.5 13.3 %all_gather.10 = f32[1024,128]{0,1:T(8,128)S(1)} all-gather(f32[128,128]{0,1:T(8,128)S(1)} %multiply_add_fusion.6), channel_id=1, replica_groups=mesh['wide'=16,'narrow'=8] {'narrow'}, dimensions={0}, use_global_device_ids=true | all-gather | bytes 589824 | tf_op jit(solution)/shard_map/all_gather | solution.py:153
  268.6 6.3 %collective-permute-start.8 = (f32[64,128]{0,1:T(8,128)S(1)}, f32[64,128]{0,1:T(8,128)S(1)}, u32[]{:S(2)}, u32[]{:S(2)}) collective-permute-start(f32[64,128]{0,1:T(8,128)S(1)} %copy.134), channel_id=1, source_target_pairs={{16,0},{24,8},{32,16},{40,24},{48,32},{56,40},{64,48},{72,56},{80,... | collective-permute-start | bytes 98312 | tf_op jit(solution)/shard_map/ppermute | solution.py:16
  275.0 4.5 collective-permute-start.9
  290.3 13.1 %all_gather.11 = f32[1024,128]{0,1:T(8,128)S(1)} all-gather(f32[128,128]{0,1:T(8,128)S(1)} %multiply_add_fusion.5), channel_id=1, replica_groups=mesh['wide'=16,'narrow'=8] {'narrow'}, dimensions={0}, use_global_device_ids=true | all-gather | bytes 589824 | tf_op jit(solution)/shard_map/all_gather | solution.py:153
  303.7 21.1 %gather_fusion.10 = f32[6144,128]{1,0:T(8,128)} fusion(f32[1024,128]{1,0:T(8,128)S(1)} %copy.121, s32[6144]{0:T(1024)S(1)} %copy-done.24), kind=kCustom, calls=%fused_computation.10 | custom fusion | bytes 6316032 | tf_op jit(solution)/shard_map/gather | solution.py:78
  329.7 4.9 %collective-permute-start.12 = (f32[3,96,128]{2,1,0:T(8,128)S(1)}, f32[3,96,128]{2,1,0:T(8,128)S(1)}, u32[]{:S(2)}, u32[]{:S(2)}) collective-permute-start(f32[3,96,128]{2,1,0:T(8,128)S(1)} %pad_maximum_fusion.8), channel_id=1, source_target_pairs={{1,0},{2,1},{3,2},{4,3},{5,4},{6,5},{7,6},{9,8},{10,9},{11,10},{12... | collective-permute-start | bytes 442376 | tf_op jit(solution)/shard_map/ppermute | solution.py:16
  334.6 6.5 %fusion.38 = f32[8192,128]{1,0:T(8,128)} fusion(f32[8192,128]{1,0:T(8,128)} %copy-done.4, f32[4,384,128]{2,1,0:T(8,128)} %param.38), kind=kOutput, calls=%fused_computation.100 | convolution fusion | flops 1610612736 | bytes 8454144 | tf_op jit(solution)/shard_map/dot_general | solution.py:20
  341.1 27.8 %gather_fusion.13 = f32[8192,128]{1,0:T(8,128)} fusion(f32[2048,128]{1,0:T(8,128)S(1)} %copy.123, s32[8192]{0:T(1024)S(1)} %copy-done.19), kind=kCustom, calls=%fused_computation.13 | custom fusion | bytes 8421376 | tf_op jit(solution)/shard_map/gather | solution.py:46
  371.0 4.5 collective-permute-done.13
  375.5 5.4 %collective-permute-start.14 = (f32[3,96,128]{2,1,0:T(8,128)S(1)}, f32[3,96,128]{2,1,0:T(8,128)S(1)}, u32[]{:S(2)}, u32[]{:S(2)}) collective-permute-start(f32[3,96,128]{2,1,0:T(8,128)S(1)} %pad_maximum_fusion.10), channel_id=1, source_target_pairs={{8,0},{16,8},{24,16},{32,24},{40,32},{48,40},{56,48},{64,56},{72,6... | collective-permute-start | bytes 442376 | tf_op jit(solution)/shard_map/ppermute | solution.py:16
  382.8 3.6 fusion.40
  386.4 3.6 collective-permute-done.15
  393.3 28.1 %gather_fusion.12 = f32[8192,128]{1,0:T(8,128)} fusion(f32[2816,128]{1,0:T(8,128)S(1)} %copy.125, s32[8192]{0:T(1024)S(1)} %copy-done.17), kind=kCustom, calls=%fused_computation.12 | custom fusion | bytes 8421376 | tf_op jit(solution)/shard_map/gather | solution.py:44
  421.4 6.3 %convolution_add_fusion.1 = f32[8192,128]{1,0:T(8,128)S(1)} fusion(f32[8192,128]{1,0:T(8,128)} %fusion.38, f32[8192,128]{1,0:T(8,128)} %gather_fusion.12, f32[4,384,128]{2,1,0:T(8,128)} %param.38), kind=kOutput, calls=%fused_computation.16 | convolution fusion | flops 1611661312 | bytes 12648448 | tf_op jit(solution)/shard_map/dot_general | solution.py:20
  427.7 4.4 fusion
  432.1 4.4 fusion.133
  439.0 4.8 %multiply_add_fusion = f32[8192,128]{1,0:T(8,128)S(1)} fusion(f32[8192,128]{1,0:T(8,128)S(1)} %copy-done.5, f32[8192,128]{1,0:T(8,128)S(1)} %get-tuple-element.63, f32[8192]{0:T(1024)S(1)} %add_rsqrt_fusion, f32[8192]{0:T(1024)S(1)} %broadcast_multiply_fusion), kind=kLoop, calls=%fused_computation.20 | loop fusion | flops 3145728 | bytes 12648448 | tf_op jit(solution)/shard_map/add | solution.py:47
  (252 shorter events, 112.5 us)
Async XLA Ops:
  7.2 81.6 %copy-start = (f32[4096,128]{1,0:T(8,128)S(1)}, f32[4096,128]{1,0:T(8,128)}, u32[]{:S(2)}) copy-start(f32[4096,128]{1,0:T(8,128)} %param.26) | copy-start | bytes 6291460
  7.2 197.1 %reduce-scatter.2.cloned.1.call-start = ((), (), s32[]{:S(2)}) async-start(), calls=%async_computation.1 | async-start | bytes 589824 | tf_op jit(solution)/shard_map/reduce_scatter | solution.py:147
  11.6 20.8 %collective-permute-start = (f32[3,96,128]{2,1,0:T(8,128)S(1)}, f32[3,96,128]{2,1,0:T(8,128)}, u32[]{:S(2)}, u32[]{:S(2)}) collective-permute-start(f32[3,96,128]{2,1,0:T(8,128)S(1)} %pad_maximum_fusion.4), channel_id=1, source_target_pairs={{1,0},{2,1},{3,2},{4,3},{5,4},{6,5},{7,6},{9,8},{10,9},{11,10},{12... | collective-permute-start | bytes 442376 | tf_op jit(solution)/shard_map/ppermute | solution.py:16
  14.2 19.0 %collective-permute-start.1 = (f32[3,96,128]{2,1,0:T(8,128)}, f32[3,96,128]{2,1,0:T(8,128)}, u32[]{:S(2)}, u32[]{:S(2)}) collective-permute-start(f32[3,96,128]{2,1,0:T(8,128)} %pad_maximum_fusion.5), channel_id=1, source_target_pairs={{0,1},{1,2},{2,3},{3,4},{4,5},{5,6},{6,7},{8,9},{9,10},{10,11},{11... | collective-permute-start | bytes 442376 | tf_op jit(solution)/shard_map/ppermute | solution.py:16
  17.4 72.6 %copy-start.16 = (s32[8192]{0:T(1024)}, s32[8192]{0:T(1024)S(1)}, u32[]{:S(2)}) copy-start(s32[8192]{0:T(1024)S(1)} %fusion.107) | copy-start | bytes 98308
  18.2 28.9 %copy-start.18 = (s32[8192]{0:T(1024)}, s32[8192]{0:T(1024)S(1)}, u32[]{:S(2)}) copy-start(s32[8192]{0:T(1024)S(1)} %fusion.108) | copy-start | bytes 98308
  35.5 53.4 %collective-permute-start.2 = (f32[3,96,128]{2,1,0:T(8,128)}, f32[3,96,128]{2,1,0:T(8,128)}, u32[]{:S(2)}, u32[]{:S(2)}) collective-permute-start(f32[3,96,128]{2,1,0:T(8,128)} %pad_maximum_fusion.6), channel_id=1, source_target_pairs={{8,0},{16,8},{24,16},{32,24},{40,32},{48,40},{56,48},{64,56},{72,6... | collective-permute-start | bytes 442376 | tf_op jit(solution)/shard_map/ppermute | solution.py:16
  42.3 46.5 %collective-permute-start.3 = (f32[3,96,128]{2,1,0:T(8,128)}, f32[3,96,128]{2,1,0:T(8,128)}, u32[]{:S(2)}, u32[]{:S(2)}) collective-permute-start(f32[3,96,128]{2,1,0:T(8,128)} %pad_maximum_fusion.7), channel_id=1, source_target_pairs={{0,8},{8,16},{16,24},{24,32},{32,40},{40,48},{48,56},{56,64},{64,7... | collective-permute-start | bytes 442376 | tf_op jit(solution)/shard_map/ppermute | solution.py:16
  45.8 94.6 %copy-start.14 = (s32[16,512]{1,0:T(8,128)}, s32[16,512]{1,0:T(8,128)S(1)}, u32[]{:S(2)}) copy-start(s32[16,512]{1,0:T(8,128)S(1)} %eq.49) | copy-start | bytes 98308
  47.1 27.9 %copy-start.45 = (u32[128]{0:T(128)S(1)}, u32[128]{0:T(128)}, u32[]{:S(2)}) copy-start(u32[128]{0:T(128)} %constant.114) | copy-start | bytes 1540
  174.8 44.2 %copy-start.38 = (f32[128]{0:T(128)}, f32[128]{0:T(128)S(1)}, u32[]{:S(2)}) copy-start(f32[128]{0:T(128)S(1)} %dynamic-slice_add_fusion) | copy-start | bytes 1540
  175.1 43.9 %copy-start.32 = (s32[1024]{0:T(1024)}, s32[1024]{0:T(1024)S(1)}, u32[]{:S(2)}) copy-start(s32[1024]{0:T(1024)S(1)} %pad_clamp_fusion.2) | copy-start | bytes 12292
  176.5 60.4 %copy-start.35 = (s32[1024]{0:T(1024)}, s32[1024]{0:T(1024)S(1)}, u32[]{:S(2)}) copy-start(s32[1024]{0:T(1024)S(1)} %pad_clamp_fusion) | copy-start | bytes 12292
  219.8 21.8 %copy-start.12 = (f32[512,128]{1,0:T(8,128)S(1)}, f32[512,128]{1,0:T(8,128)}, u32[]{:S(2)}) copy-start(f32[512,128]{1,0:T(8,128)} %fusion.60) | copy-start | bytes 786436
  219.9 17.0 %collective-permute-start.4 = (f32[64,128]{0,1:T(8,128)S(1)}, f32[64,128]{0,1:T(8,128)S(1)}, u32[]{:S(2)}, u32[]{:S(2)}) collective-permute-start(f32[64,128]{0,1:T(8,128)S(1)} %copy.130), channel_id=1, source_target_pairs={{16,0},{24,8},{32,16},{40,24},{48,32},{56,40},{64,48},{72,56},{80,... | collective-permute-start | bytes 98312 | tf_op jit(solution)/shard_map/ppermute | solution.py:16
  225.3 11.6 %collective-permute-start.5 = (f32[64,128]{0,1:T(8,128)S(1)}, f32[64,128]{0,1:T(8,128)S(1)}, u32[]{:S(2)}, u32[]{:S(2)}) collective-permute-start(f32[64,128]{0,1:T(8,128)S(1)} %copy.131), channel_id=1, source_target_pairs={{8,0},{16,8},{24,16},{32,24},{40,32},{48,40},{56,48},{64,56},{72,6... | collective-permute-start | bytes 98312 | tf_op jit(solution)/shard_map/ppermute | solution.py:16
  228.4 8.5 %collective-permute-start.6 = (f32[64,128]{0,1:T(8,128)S(1)}, f32[64,128]{0,1:T(8,128)S(1)}, u32[]{:S(2)}, u32[]{:S(2)}) collective-permute-start(f32[64,128]{0,1:T(8,128)S(1)} %copy.132), channel_id=1, source_target_pairs={{0,8},{8,16},{16,24},{24,32},{32,40},{40,48},{48,56},{56,64},{64,7... | collective-permute-start | bytes 98312 | tf_op jit(solution)/shard_map/ppermute | solution.py:16
  231.4 8.6 %collective-permute-start.7 = (f32[64,128]{0,1:T(8,128)S(1)}, f32[64,128]{0,1:T(8,128)S(1)}, u32[]{:S(2)}, u32[]{:S(2)}) collective-permute-start(f32[64,128]{0,1:T(8,128)S(1)} %copy.133), channel_id=1, source_target_pairs={{0,16},{8,24},{16,32},{24,40},{32,48},{40,56},{48,64},{56,72},{64,... | collective-permute-start | bytes 98312 | tf_op jit(solution)/shard_map/ppermute | solution.py:16
  240.3 22.7 %copy-start.33 = (s32[1024]{0:T(1024)S(1)}, s32[1024]{0:T(1024)}, u32[]{:S(2)}) copy-start(s32[1024]{0:T(1024)} %copy-done.32) | copy-start | bytes 12292
  242.7 38.0 %copy-start.36 = (s32[1024]{0:T(1024)S(1)}, s32[1024]{0:T(1024)}, u32[]{:S(2)}) copy-start(s32[1024]{0:T(1024)} %copy-done.35) | copy-start | bytes 12292
  262.8 19.9 %copy-start.34 = (s32[1024]{0:T(1024)S(1)}, s32[1024]{0:T(1024)}, u32[]{:S(2)}) copy-start(s32[1024]{0:T(1024)} %pad_clamp_fusion.1) | copy-start | bytes 12292
  263.9 18.5 %collective-permute-start.10 = (f32[64,128]{0,1:T(8,128)S(1)}, f32[64,128]{0,1:T(8,128)S(1)}, u32[]{:S(2)}, u32[]{:S(2)}) collective-permute-start(f32[64,128]{0,1:T(8,128)S(1)} %copy.136), channel_id=1, source_target_pairs={{0,8},{8,16},{16,24},{24,32},{32,40},{40,48},{48,56},{56,64},{64,7... | collective-permute-start | bytes 98312 | tf_op jit(solution)/shard_map/ppermute | solution.py:16
  266.5 15.9 %collective-permute-start.11 = (f32[64,128]{0,1:T(8,128)S(1)}, f32[64,128]{0,1:T(8,128)S(1)}, u32[]{:S(2)}, u32[]{:S(2)}) collective-permute-start(f32[64,128]{0,1:T(8,128)S(1)} %copy.137), channel_id=1, source_target_pairs={{0,16},{8,24},{16,32},{24,40},{32,48},{40,56},{48,64},{56,72},{64,... | collective-permute-start | bytes 98312 | tf_op jit(solution)/shard_map/ppermute | solution.py:16
  268.6 13.8 %collective-permute-start.8 = (f32[64,128]{0,1:T(8,128)S(1)}, f32[64,128]{0,1:T(8,128)S(1)}, u32[]{:S(2)}, u32[]{:S(2)}) collective-permute-start(f32[64,128]{0,1:T(8,128)S(1)} %copy.134), channel_id=1, source_target_pairs={{16,0},{24,8},{32,16},{40,24},{48,32},{56,40},{64,48},{72,56},{80,... | collective-permute-start | bytes 98312 | tf_op jit(solution)/shard_map/ppermute | solution.py:16
  275.0 7.4 %collective-permute-start.9 = (f32[64,128]{0,1:T(8,128)S(1)}, f32[64,128]{0,1:T(8,128)S(1)}, u32[]{:S(2)}, u32[]{:S(2)}) collective-permute-start(f32[64,128]{0,1:T(8,128)S(1)} %copy.135), channel_id=1, source_target_pairs={{8,0},{16,8},{24,16},{32,24},{40,32},{48,40},{56,48},{64,56},{72,6... | collective-permute-start | bytes 98312 | tf_op jit(solution)/shard_map/ppermute | solution.py:16
  282.8 20.9 %copy-start.24 = (s32[6144]{0:T(1024)S(1)}, s32[6144]{0:T(1024)}, u32[]{:S(2)}) copy-start(s32[6144]{0:T(1024)} %broadcast_clamp_fusion) | copy-start | bytes 73732
  303.7 21.1 %copy-start.3 = (f32[1024,128]{1,0:T(8,128)}, f32[1024,128]{1,0:T(8,128)S(1)}, u32[]{:S(2)}) copy-start(f32[1024,128]{1,0:T(8,128)S(1)} %copy.121) | copy-start | bytes 1572868
  303.7 21.1 %copy-start.25 = (f32[3,2048]{1,0:T(4,128)S(1)}, f32[3,2048]{1,0:T(4,128)}, u32[]{:S(2)}) copy-start(f32[3,2048]{1,0:T(4,128)} %get-tuple-element.11) | copy-start | bytes 73732
  329.7 41.2 %collective-permute-start.12 = (f32[3,96,128]{2,1,0:T(8,128)S(1)}, f32[3,96,128]{2,1,0:T(8,128)S(1)}, u32[]{:S(2)}, u32[]{:S(2)}) collective-permute-start(f32[3,96,128]{2,1,0:T(8,128)S(1)} %pad_maximum_fusion.8), channel_id=1, source_target_pairs={{1,0},{2,1},{3,2},{4,3},{5,4},{6,5},{7,6},{9,8},{10,9},{11,10},{12... | collective-permute-start | bytes 442376 | tf_op jit(solution)/shard_map/ppermute | solution.py:16
  369.0 6.5 %collective-permute-start.13 = (f32[3,96,128]{2,1,0:T(8,128)S(1)}, f32[3,96,128]{2,1,0:T(8,128)S(1)}, u32[]{:S(2)}, u32[]{:S(2)}) collective-permute-start(f32[3,96,128]{2,1,0:T(8,128)S(1)} %pad_maximum_fusion.9), channel_id=1, source_target_pairs={{0,1},{1,2},{2,3},{3,4},{4,5},{5,6},{6,7},{8,9},{9,10},{10,11},{11... | collective-permute-start | bytes 442376 | tf_op jit(solution)/shard_map/ppermute | solution.py:16
  375.5 10.9 %collective-permute-start.14 = (f32[3,96,128]{2,1,0:T(8,128)S(1)}, f32[3,96,128]{2,1,0:T(8,128)S(1)}, u32[]{:S(2)}, u32[]{:S(2)}) collective-permute-start(f32[3,96,128]{2,1,0:T(8,128)S(1)} %pad_maximum_fusion.10), channel_id=1, source_target_pairs={{8,0},{16,8},{24,16},{32,24},{40,32},{48,40},{56,48},{64,56},{72,6... | collective-permute-start | bytes 442376 | tf_op jit(solution)/shard_map/ppermute | solution.py:16
  380.9 9.1 %collective-permute-start.15 = (f32[3,96,128]{2,1,0:T(8,128)S(1)}, f32[3,96,128]{2,1,0:T(8,128)S(1)}, u32[]{:S(2)}, u32[]{:S(2)}) collective-permute-start(f32[3,96,128]{2,1,0:T(8,128)S(1)} %pad_maximum_fusion.11), channel_id=1, source_target_pairs={{0,8},{8,16},{16,24},{24,32},{32,40},{40,48},{48,56},{56,64},{64,7... | collective-permute-start | bytes 442376 | tf_op jit(solution)/shard_map/ppermute | solution.py:16
  (31 other events, 219.1 us)
Sparse Core Ops, SparseCore 0:
  174.2 30.0 reduce-scatter.1
where the time goes:
time: 469 us; the launch traced here: 462 us
  local copies, waits for them, and re-layouts  176 us (38%)
  matrix products  89.5 us (19%)
  starting transfers between devices  55.7 us (12%)
  blocking collectives  52.6 us (11%)
  other arithmetic  35.7 us (8%)
  waiting for transfers between devices  35.6 us (8%)
  between operations  16.3 us (3%)
    dot_general x28, matrix products, matmul(): jnp.dot(operand, weights, precision=highest, preferred_element_type=jnp.f...  75.5 us
    gather x4, local copies, waits for them, and re-layouts, graph_step(): hidden = hidden + matmul(receivers[target], edge_in[2 * latent:])  58.4 us
    gather x4, local copies, waits for them, and re-layouts, graph_step(): source_rows[sender]  58.2 us
    ppermute x16, starting transfers between devices, from_behind(): return lax.ppermute(block, axis, route)  55.7 us
    all_gather x3, blocking collectives, gather_rows(): return lax.all_gather(share_rows, 'narrow', axis=0, tiled=True)  40 us
    reduce_scatter x1, waiting for transfers between devices, local(): lax.psum_scatter(numer, 'narrow', scatter_dimension=0, tiled=True)  24.5 us
    gather x1, local copies, waits for them, and re-layouts, prolong_rows(): picked = owner_rows[index_rows]  21.1 us
    gather x1, local copies, waits for them, and re-layouts, restrict_partial(): picked = fine_rows[source].reshape(blocks, TILE, latent)  17.8 us
  transfers between devices with their start and end apart: 17, of which 4 were waited for; matrix products, arithmetic and copies ran while one was open for 21% of the time, Pallas kernels for 0%

commit v1 on v0

v1 whole, which is shorter than its diff:
```python
import functools

import jax
import jax.numpy as jnp
from jax import lax
from jax.experimental import pallas as pl
from jax.experimental.pallas import tpu as pltpu
from jax.sharding import PartitionSpec as P

MESH = pl.DeviceIdType.MESH
f32, bf16, i32 = jnp.float32, jnp.bfloat16, jnp.int32
LANES = 128
FINE_SIDES = ((-1, -1), (-1, 0), (-1, 1), (0, -1), (0, 1), (1, -1), (1, 0), (1, 1))
COARSE_SIDES = (-2, -1, 1, 2)
EDGE_OWN, EDGE_FROM, EDGE_TO, EDGE_OUT, NODE_OWN, NODE_SUM, NODE_OUT = range(7)


def halves(values):
    high = values.astype(bf16)
    return high, (values - high.astype(f32)).astype(bf16)


def wide_halves(values):
    return jnp.concatenate(halves(values), axis=1)


def fold(product):
    return product[:, :LANES] + product[:, LANES:]


def dot(left, right):
    return jnp.dot(left, right, preferred_element_type=f32)


def mm(values, weight):
    return fold(dot(wide_halves(values), weight))


def normed(centered):
    return centered * lax.rsqrt(jnp.mean(centered * centered, axis=-1, keepdims=True) + 1e-05)


def as_columns(row):
    return jnp.broadcast_to(row, (LANES, LANES)).T


def lookup(levels, table):
    found = jnp.zeros(levels.shape, f32)
    for level in range(table.shape[0]):
        found = jnp.where(levels == level, table[level], found)
    return found


def sub_iota(shape):
    return lax.broadcasted_iota(i32, shape, 0)


def lane_iota(shape):
    return lax.broadcasted_iota(i32, shape, 1)


def span(start, size):
    return pl.ds(pl.multiple_of(start, size), size)


def take_rows(index_of, count, table, out, out_start, unroll):
    def one(j, carry):
        out[pl.ds(out_start + j, 1), :] = table[pl.ds(index_of(j), 1), :]
        return carry

    lax.fori_loop(0, count, one, 0, unroll=unroll)


def kernel(
    sizes,
    sender, send, csender, csend, rsource, rtile, rtable, ptable,
    foff, coff, roff, rlevel, pindex, plevel,
    x_in, e_in, ce_in, ew1, ew2, nw1, nw2,
    out, cout,
    x, e, base, table, xc, xv, agg, ga, gb, ohg, ohs, wd,
    r_ew1, r_ew2, r_nw1, r_nw2,
    hout1, hin1, hout2, hin2,
    scale, roh, rsel, picked, contrib, rs_out, rs_in, dd_out, dd_in,
    cx, ce, cbase, ctable1, ctable2, cohg, cohs, chout1, chout2, chin1, chin2, cxc, cxv, cg, cfull,
    amat,
    local_sem, h1s, h1r, h2s, h2r, rss, rsr, dds, ddr, a1s, a1r, a2s, a2r, a3s, a3r,
    c1s, c1r, c2s, c2r,
):
    W, N = sizes
    w, n = lax.axis_index("wide"), lax.axis_index("narrow")
    nodes, slots = x.shape[0], e.shape[0]
    halo = send.shape[2]
    tiles = nodes // LANES
    per_tile = slots // tiles
    unit = per_tile // 2
    cown = cfull.shape[0]
    chalo = csend.shape[2]
    cslots = ce.shape[0]
    blocks = rsource.shape[0] // LANES

    def inside(dw, dn):
        return (w + dw >= 0) & (w + dw < W) & (n + dn >= 0) & (n + dn < N)

    def remote(src, dst, send_sem, recv_sem, where):
        return pltpu.make_async_remote_copy(
            src_ref=src, dst_ref=dst, send_sem=send_sem, recv_sem=recv_sem,
            device_id=where, device_id_type=MESH,
        )

    def peer(d):
        return lax.rem(n + d, N)

    own_edges = cslots * n
    loads = [
        pltpu.make_async_copy(x_in, x, local_sem.at[0]),
        pltpu.make_async_copy(ew1, r_ew1, local_sem.at[1]),
        pltpu.make_async_copy(ew2, r_ew2, local_sem.at[2]),
        pltpu.make_async_copy(nw1, r_nw1, local_sem.at[3]),
        pltpu.make_async_copy(nw2, r_nw2, local_sem.at[4]),
        pltpu.make_async_copy(e_in, e, local_sem.at[5]),
        pltpu.make_async_copy(ce_in.at[span(own_edges, cslots)], ce, local_sem.at[6]),
    ]
    for load in loads:
        load.start()

    barrier = pltpu.get_barrier_semaphore()
    others = [(dw, dn) for dw, dn in FINE_SIDES if dw] + [(-2, 0), (2, 0)]
    for d in range(1, N):
        pl.semaphore_signal(barrier, inc=1, device_id=(w, peer(d)), device_id_type=MESH)
    expected = i32(N - 1)
    for dw, dn in others:
        @pl.when(inside(dw, dn))
        def _():
            pl.semaphore_signal(barrier, inc=1, device_id=(w + dw, n + dn), device_id_type=MESH)
        expected = expected + inside(dw, dn).astype(i32)

    def fine_copy(k, hout, hin, ss, rs, where):
        return remote(hout.at[k], hin.at[k], ss.at[k], rs.at[k], where)

    def fine_start(k, hout, hin, ss, rs):
        dw, dn = FINE_SIDES[k]

        @pl.when(inside(dw, dn))
        def _():
            fine_copy(k, hout, hin, ss, rs, (w + dw, n + dn)).start()

    def fine_arrive(k, hout, hin, ss, rs):
        dw, dn = FINE_SIDES[k]

        @pl.when(inside(-dw, -dn))
        def _():
            fine_copy(k, hout, hin, ss, rs, (w - dw, n - dn)).wait_recv()

        @pl.when(jnp.logical_not(inside(-dw, -dn)))
        def _():
            hin[k] = jnp.zeros(hin.shape[1:], f32)

    def fine_sent(k, hout, hin, ss, rs):
        dw, dn = FINE_SIDES[k]

        @pl.when(inside(dw, dn))
        def _():
            fine_copy(k, hout, hin, ss, rs, (w + dw, n + dn)).wait_send()

    def pick_halo(k, hout):
        take_rows(lambda j: send[0, k, j], halo, x, hout.at[k], 0, 16)

    loads[0].wait()
    for k in range(8):
        pick_halo(k, hout1)
    pl.semaphore_wait(barrier, expected)
    for k in range(8):
        fine_start(k, hout1, hin1, h1s, h1r)

    for load in loads[1:5]:
        load.wait()

    def put_weight(section, place, value):
        high, low = halves(value)
        wide = jnp.concatenate([high, low], axis=1)
        wd[section * 7 + place] = jnp.concatenate([wide, wide], axis=0)

    def center(value):
        return value - jnp.mean(value, axis=1, keepdims=True)

    def prepare(s):
        put_weight(s, EDGE_OWN, r_ew1[s, 0:128, :])
        put_weight(s, EDGE_FROM, r_ew1[s, 128:256, :])
        put_weight(s, EDGE_TO, r_ew1[s, 256:384, :])
        put_weight(s, EDGE_OUT, center(r_ew2[s]))
        put_weight(s, NODE_OWN, r_nw1[s, 0:128, :])
        put_weight(s, NODE_SUM, r_nw1[s, 128:256, :])
        put_weight(s, NODE_OUT, center(r_nw2[s]))

    prepare(0)

    def weight(s, place):
        return wd[s * 7 + place]

    lanes = lane_iota((LANES, LANES))
    rows = sub_iota((LANES, LANES))
    per_block = per_tile // LANES

    def one_hots(t, carry):
        for c in range(per_block):
            row = foff[pl.ds(t * per_block + c, 1), :]
            to = as_columns(jnp.minimum(row, LANES - 1))
            ohg[span(t * per_tile + c * LANES, LANES), :] = (to == lanes).astype(f32).astype(bf16)
            ohs[span(t * LANES, LANES), c * LANES : (c + 1) * LANES] = (
                (rows == row).astype(f32).astype(bf16)
            )
        return carry

    lax.fori_loop(0, tiles, one_hots, 0)

    def fine_own(s):
        def project(b, carry):
            part = span(b * 256, 256)
            wide = wide_halves(x[part, :])
            table[part, :] = fold(dot(wide, weight(s, EDGE_FROM)))
            xc[part, :] = wide_halves(fold(dot(wide, weight(s, EDGE_TO))))
            xv[part, :] = fold(dot(wide, weight(s, NODE_OWN)))
            return carry

        lax.fori_loop(0, nodes // 256, project, 0)

    def fine_base(s):
        def one(t, carry):
            to = xc[span(t * LANES, LANES), :]
            for u in range(2):
                part = span(t * per_tile + u * unit, unit)
                base[part, :] = mm(e[part, :], weight(s, EDGE_OWN)) + fold(dot(ohg[part, :], to))
            return carry

        lax.fori_loop(0, tiles, one, 0)

    def fine_halo_in(s, hout, hin, ss, rs):
        for k in range(8):
            fine_arrive(k, hout, hin, ss, rs)
            table[nodes + k * halo : nodes + (k + 1) * halo, :] = mm(hin[k], weight(s, EDGE_FROM))

    def fine_edges_nodes(s, keep, write):
        def fill(t, u, buffer):
            start = t * per_tile + u * unit
            take_rows(lambda j: sender[start + j], unit, table, buffer, 0, UNROLL)

        def part_sum(t, u, buffer):
            part = span(t * per_tile + u * unit, unit)
            h = jnp.maximum(base[part, :] + buffer[...], 0.0)
            fresh = e[part, :] + normed(mm(h, weight(s, EDGE_OUT)))
            if keep:
                e[part, :] = fresh
            onto = ohs[span(t * LANES, LANES), u * unit : (u + 1) * unit]
            return fold(dot(onto, wide_halves(fresh)))

        fill(0, 0, ga)

        def one(t, carry):
            fill(t, 1, gb)
            total = part_sum(t, 0, ga)
            fill(jnp.minimum(t + 1, tiles - 1), 0, ga)
            agg[span(t * LANES, LANES), :] = total + part_sum(t, 1, gb)
            return carry

        lax.fori_loop(0, tiles, one, 0)

        def node(b, carry):
            part = span(b * 256, 256)
            h = jnp.maximum(xv[part, :] + mm(agg[part, :], weight(s, NODE_SUM)), 0.0)
            write(part, x[part, :] + normed(mm(h, weight(s, NODE_OUT))))
            return carry

        lax.fori_loop(0, nodes // 256, node, 0)

    fine_own(0)
    loads[5].wait()
    fine_base(0)
    fine_halo_in(0, hout1, hin1, h1s, h1r)

    def keep_nodes(part, value):
        x[part, :] = value

    fine_edges_nodes(0, True, keep_nodes)

    scale[...] = lookup(rlevel[...], rtable)

    def restrict_block(b, carry):
        take_rows(lambda j: rsource[b * LANES + j], LANES, x, picked, 0, UNROLL)
        row = roff[pl.ds(b, 1), :]
        hit = rows == row
        roh[:, span(b * LANES, LANES)] = hit.astype(f32).astype(bf16)
        left = wide_halves(jnp.where(hit, scale[pl.ds(b, 1), :], 0.0))
        right = wide_halves(picked[...])
        contrib[b] = fold(dot(left, jnp.concatenate([right, right], axis=0)))
        return carry

    lax.fori_loop(0, blocks, restrict_block, 0)

    def restrict_tile(t):
        def add(b, total):
            return total + contrib[b] * (rtile[b] == t).astype(f32)

        rs_out[t] = lax.fori_loop(0, blocks, add, jnp.zeros((LANES, LANES), f32), unroll=4)

    def share_copy(d, toward):
        return remote(rs_out.at[peer(d)], rs_in.at[d], rss.at[d], rsr.at[d], (w, toward))

    for d in range(1, N):
        restrict_tile(peer(d))
        share_copy(d, peer(d)).start()

    def select_block(b, carry):
        kept = jnp.where(sub_iota((8, LANES)) == rtile[b], scale[pl.ds(b, 1), :], 0.0)
        high = kept.astype(bf16).astype(f32)
        rsel[:, span(b * LANES, LANES)] = jnp.concatenate([high, kept - high], axis=0).astype(bf16)
        return carry

    lax.fori_loop(0, blocks, select_block, 0)
    weights = lax.dot_general(
        rsel[...], roh[...], (((1,), (1,)), ((), ())), preferred_element_type=f32
    )
    weights = weights[0:8] + weights[8:16]
    for t in range(N):
        dd_out[t] = jnp.broadcast_to(weights[t : t + 1], (8, LANES))

    def weight_copy(d, toward):
        return remote(dd_out.at[peer(d)], dd_in.at[d], dds.at[d], ddr.at[d], (w, toward))

    for d in range(1, N):
        weight_copy(d, peer(d)).start()
    restrict_tile(n)

    prepare(1)

    def prolong_block(b, carry):
        part = span(b * LANES, LANES)
        raw = [lookup(plevel[k : k + 1, part], ptable) for k in range(3)]
        total = raw[0] + raw[1] + raw[2]
        places = [as_columns(pindex[k : k + 1, part]) for k in range(3)]
        amounts = [as_columns(r / total) for r in raw]
        for c in range(cown // LANES):
            value = jnp.zeros((LANES, LANES), f32)
            for k in range(3):
                value = value + jnp.where(places[k] == lanes + c * LANES, amounts[k], 0.0)
            high, low = halves(value)
            amat[part, c * LANES : (c + 1) * LANES] = high
            amat[part, cown + c * LANES : cown + (c + 1) * LANES] = low
        return carry

    def prolong_weights(part):
        lax.fori_loop(part * tiles // 4, (part + 1) * tiles // 4, prolong_block, 0)

    crow = n * (cslots // LANES)
    for c in range(cslots // LANES):
        row = coff[pl.ds(crow + c, 1), :]
        cohg[c * LANES : (c + 1) * LANES, :] = (
            (as_columns(jnp.minimum(row, LANES - 1)) == lanes).astype(f32).astype(bf16)
        )
        cohs[:, c * LANES : (c + 1) * LANES] = (rows == row).astype(f32).astype(bf16)
    loads[6].wait()
    prolong_weights(0)

    numer = rs_out[n]
    denom = dd_out[n]
    for d in range(1, N):
        share_copy(d, peer(N - d)).wait_recv()
        weight_copy(d, peer(N - d)).wait_recv()
        numer = numer + rs_in[d]
        denom = denom + dd_in[d]
    cx[...] = numer / (1.0 + as_columns(denom[0:1]))

    own = span(n * LANES, LANES)

    def gather_copy(d, rows_ref, ss, rs, source, toward):
        place = rows_ref.at[span(source * LANES, LANES)]
        return remote(place, place, ss.at[d], rs.at[d], (w, toward))

    def gather_start(rows_ref, ss, rs):
        for d in range(1, N):
            gather_copy(d, rows_ref, ss, rs, n, peer(d)).start()

    def gather_arrive(rows_ref, ss, rs):
        for d in range(1, N):
            gather_copy(d, rows_ref, ss, rs, peer(N - d), peer(N - d)).wait_recv()

    def gather_sent(rows_ref, ss, rs):
        for d in range(1, N):
            gather_copy(d, rows_ref, ss, rs, n, peer(d)).wait_send()

    def coarse_copy(k, chin, chout, ss, rs, toward):
        return remote(chout.at[k], chin.at[k], ss.at[k], rs.at[k], (toward, n))

    def coarse_step(s, ctable, chin, chout, gs, gr, cs, cr, keep, meanwhile):
        wide = wide_halves(cx[...])
        ctable[own, :] = fold(dot(wide, weight(s, EDGE_FROM)))
        gather_start(ctable, gs, gr)
        cxc[...] = wide_halves(fold(dot(wide, weight(s, EDGE_TO))))
        cxv[...] = fold(dot(wide, weight(s, NODE_OWN)))
        cbase[...] = mm(ce[...], weight(s, EDGE_OWN)) + fold(dot(cohg[...], cxc[...]))
        meanwhile[0]()
        gather_arrive(ctable, gs, gr)
        for k, dw in enumerate(COARSE_SIDES):
            take_rows(lambda j: csend[0, k, j], chalo, ctable, chout.at[k], 0, 16)

            @pl.when(inside(dw, 0))
            def _():
                coarse_copy(k, chin, chout, cs, cr, w + dw).start()

        meanwhile[1]()
        for k, dw in enumerate(COARSE_SIDES):
            @pl.when(inside(-dw, 0))
            def _():
                coarse_copy(k, chin, chout, cs, cr, w - dw).wait_recv()
                ctable[cown + k * chalo : cown + (k + 1) * chalo, :] = chin[k]

            @pl.when(jnp.logical_not(inside(-dw, 0)))
            def _():
                ctable[cown + k * chalo : cown + (k + 1) * chalo, :] = jnp.zeros((chalo, LANES), f32)

        take_rows(lambda j: csender[n * cslots + j], cslots, ctable, cg, 0, UNROLL)
        h = jnp.maximum(cbase[...] + cg[...], 0.0)
        fresh = ce[...] + normed(mm(h, weight(s, EDGE_OUT)))
        if keep:
            ce[...] = fresh
        total = fold(dot(cohs[...], wide_halves(fresh)))
        h = jnp.maximum(cxv[...] + mm(total, weight(s, NODE_SUM)), 0.0)
        cx[...] = cx[...] + normed(mm(h, weight(s, NODE_OUT)))

    coarse_step(1, ctable1, chin1, chout1, a1s, a1r, c1s, c1r, True,
                (lambda: prolong_weights(1), lambda: prepare(2)))
    coarse_step(2, ctable2, chin2, chout2, a2s, a2r, c2s, c2r, False,
                (lambda: prolong_weights(2), lambda: prolong_weights(3)))

    cfull[own, :] = cx[...]
    gather_start(cfull, a3s, a3r)
    prepare(3)
    gather_arrive(cfull, a3s, a3r)
    cstore = pltpu.make_async_copy(cfull, cout, local_sem.at[7])
    cstore.start()

    cwide = wide_halves(cfull[...])

    def prolong_rows(b, carry):
        part = span(b * 256, 256)
        total = dot(amat[part, 0:cown], cwide) + dot(amat[part, cown:], cwide)
        x[part, :] = x[part, :] + fold(total)
        return carry

    lax.fori_loop(0, nodes // 256, prolong_rows, 0)

    for k in range(8):
        pick_halo(k, hout2)
        fine_start(k, hout2, hin2, h2s, h2r)
    fine_own(3)
    fine_base(3)
    fine_halo_in(3, hout2, hin2, h2s, h2r)

    def write_nodes(part, value):
        agg[part, :] = value

    fine_edges_nodes(3, False, write_nodes)
    store = pltpu.make_async_copy(agg, out, local_sem.at[0])
    store.start()

    for k in range(8):
        fine_sent(k, hout1, hin1, h1s, h1r)
        fine_sent(k, hout2, hin2, h2s, h2r)
    for d in range(1, N):
        share_copy(d, peer(d)).wait_send()
        weight_copy(d, peer(d)).wait_send()
    gather_sent(ctable1, a1s, a1r)
    gather_sent(ctable2, a2s, a2r)
    gather_sent(cfull, a3s, a3r)
    for k, dw in enumerate(COARSE_SIDES):
        @pl.when(inside(dw, 0))
        def _():
            coarse_copy(k, chin1, chout1, c1s, c1r, w + dw).wait_send()
            coarse_copy(k, chin2, chout2, c2s, c2r, w + dw).wait_send()
    cstore.wait()
    store.wait()


UNROLL = 32


def local(
    W, N,
    fine_nodes, fine_edges, fine_sender, fine_offset, fine_send,
    coarse_edges, coarse_sender, coarse_offset, coarse_send,
    restrict_source, restrict_offset, restrict_tile, restrict_weight,
    prolong_index, prolong_weight, restrict_table, prolong_table,
    edge_w1, edge_w2, node_w1, node_w2,
):
    nodes, slots = fine_nodes.shape[0], fine_edges.shape[0]
    halo, chalo = fine_send.shape[2], coarse_send.shape[2]
    tiles = nodes // LANES
    per_tile = slots // tiles
    cown = N * LANES
    cslots = coarse_edges.shape[0] // N
    blocks = restrict_tile.shape[0]
    smem = pl.BlockSpec(memory_space=pltpu.SMEM)
    vmem = pl.BlockSpec(memory_space=pltpu.VMEM)
    hbm = pl.BlockSpec(memory_space=pl.ANY)

    def F(*shape):
        return pltpu.VMEM(shape, f32)

    def B(*shape):
        return pltpu.VMEM(shape, bf16)

    def D(count):
        return pltpu.SemaphoreType.DMA((count,))

    row = lambda flat: flat.reshape(-1, LANES)
    return pl.pallas_call(
        functools.partial(kernel, (W, N)),
        out_shape=(
            jax.ShapeDtypeStruct((nodes, LANES), f32),
            jax.ShapeDtypeStruct((cown, LANES), f32),
        ),
        in_specs=[smem] * 8 + [vmem] * 6 + [hbm] * 7,
        out_specs=(hbm, hbm),
        scratch_shapes=[
            F(nodes, LANES), F(slots, LANES), F(slots, LANES), F(nodes + 8 * halo, LANES),
            B(nodes, 2 * LANES), F(nodes, LANES), F(nodes, LANES),
            F(per_tile // 2, LANES), F(per_tile // 2, LANES),
            B(slots, LANES), B(nodes, per_tile), B(28, 2 * LANES, 2 * LANES),
            F(*edge_w1.shape), F(*edge_w2.shape), F(*node_w1.shape), F(*node_w2.shape),
            F(8, halo, LANES), F(8, halo, LANES), F(8, halo, LANES), F(8, halo, LANES),
            F(blocks, LANES), B(LANES, blocks * LANES), B(16, blocks * LANES), F(LANES, LANES),
            F(blocks, LANES, LANES), F(N, LANES, LANES), F(N, LANES, LANES),
            F(N, 8, LANES), F(N, 8, LANES),
            F(LANES, LANES), F(cslots, LANES), F(cslots, LANES),
            F(cown + 4 * chalo, LANES), F(cown + 4 * chalo, LANES),
            B(cslots, LANES), B(LANES, cslots), F(4, chalo, LANES), F(4, chalo, LANES), F(4, chalo, LANES), F(4, chalo, LANES),
            B(LANES, 2 * LANES), F(LANES, LANES), F(cslots, LANES), F(cown, LANES),
            B(nodes, 2 * cown),
            D(8), D(8), D(8), D(8), D(8), D(N), D(N), D(N), D(N),
            D(N), D(N), D(N), D(N), D(N), D(N), D(4), D(4), D(4), D(4),
        ],
        compiler_params=pltpu.CompilerParams(
            collective_id=0, has_side_effects=True, vmem_limit_bytes=60 << 20
        ),
        name="graph_window",
    )(
        fine_sender, fine_send, coarse_sender, coarse_send, restrict_source, restrict_tile,
        restrict_table, prolong_table,
        row(fine_offset), row(coarse_offset), row(restrict_offset), row(restrict_weight),
        prolong_index, prolong_weight,
        fine_nodes, fine_edges, coarse_edges, edge_w1, edge_w2, node_w1, node_w2,
    )


def solution(mesh):
    both = ("wide", "narrow")
    placed = (
        P(both, None), P(both, None), P(both), P(both), P(both, None, None),
        P("wide", None), P("wide"), P("wide"), P("wide", None, None),
        P(both), P(both), P(both), P(both), P(None, both), P(None, both),
        P(), P(), P(), P(), P(), P(),
    )
    return jax.shard_map(
        functools.partial(local, mesh.shape["wide"], mesh.shape["narrow"]),
        mesh=mesh,
        in_specs=placed,
        out_specs=(P(both, None), P("wide", None)),
        check_vma=False,
    )
```

time: 469 us -> 155 us (0.33)
  local copies, waits for them, and re-layouts: 176 us -> 4.13 us
  Pallas kernels: 0 us -> 147 us
  matrix products: 89.5 us -> 0 us
  starting transfers between devices: 55.7 us -> 0 us
  blocking collectives: 52.6 us -> 0 us
  other arithmetic: 35.7 us -> 0 us
  waiting for transfers between devices: 35.6 us -> 0 us
  between operations: 16.3 us -> 0.65 us
    gather x14 -> x0, local copies, waits for them, and re-layouts: 161 us -> none  [the longest x4 58.4 us: graph_step(): hidden = hidden + matmul(receivers[target], edge_in[2 * latent:])]
    pallas_call x0 -> x1, Pallas kernels: none -> 147 us  [local(): pl.pallas_call(functools.partial(kernel, (W, N)), out_shape=(jax.ShapeDty...]
    dot_general x35 -> x0, matrix products: 89.5 us -> none  [the longest x28 75.5 us: matmul(): jnp.dot(operand, weights, precision=highest, preferred_element_type=jnp.f...]
    ppermute x16 -> x0, starting transfers between devices: 55.7 us -> none  [from_behind(): return lax.ppermute(block, axis, route)]
    all_gather x3 -> x0, blocking collectives: 40 us -> none  [gather_rows(): return lax.all_gather(share_rows, 'narrow', axis=0, tiled=True)]
    reduce_scatter x1 -> x0, waiting for transfers between devices: 24.5 us -> none  [local(): lax.psum_scatter(numer, 'narrow', scatter_dimension=0, tiled=True)]
    unnamed x1 -> x0, blocking collectives: 12.5 us -> none
    add x9 -> x0, other arithmetic: 12 us -> none  [the longest x3 9.72 us: graph_step(): new_edges = edge_rows + layer_norm(matmul(jax.nn.relu(hidden), edge_out))]
  transfers between devices with their start and end apart: 17 -> 0, of which waited for: 4 -> 0; matrix products, arithmetic and copies ran while one was open for 21% -> 0% of each run, Pallas kernels for 0% -> 0%
where the time goes in v1:
time: 155 us; the launch traced here: 152 us
  Pallas kernels  147 us (95%)
  local copies, waits for them, and re-layouts  4.13 us (3%)
    pallas_call x1, Pallas kernels, local(): pl.pallas_call(functools.partial(kernel, (W, N)), out_shape=(jax.ShapeDty...  147 us
    unnamed x2, local copies, waits for them, and re-layouts  4.13 us

profile of v1, /device:TPU:14, one launch (start us, length us, event | category | flops | bytes accessed | tf_op | source)
XLA Modules:
  0.0 151.6 jit_solution(2543936582066220169)
XLA Ops:
  0.6 146.8 %graph_window.1 = (f32[2048,128]{1,0:T(8,128)}, f32[1024,128]{1,0:T(8,128)}) custom-call(s32[8192]{0:T(1024)} %sender.1, s32[1,8,96]{2,1,0:T(8,128)} %send.1, s32[4096]{0:T(1024)} %csender.1, s32[1,4,64]{2,1,0:T(4,128)} %csend.1, s32[5120]{0:T(1024)} %rsource.1, s32[40]{0:T(128)} %rtile.1, f32[16]{0:T(128)} %rtable.1, f32[16]{0:T(128)} %ptable.1, ...), custom_call_target="tpu_custom_call" | custom-call | tf_op jit(solution)/shard_map/graph_window/pallas_call | solution.py:515
  147.5 2.3 %copy.25 = f32[2048,128]{1,0:T(8,128)} copy(f32[2048,128]{1,0:T(8,128)} %get-tuple-element.4) | data formatting | bytes 2097152
  149.7 1.9 %copy.26 = f32[1024,128]{1,0:T(8,128)} copy(f32[1024,128]{1,0:T(8,128)} %get-tuple-element.5) | data formatting | bytes 1048576

commit v2 on v1

v2 whole, which is shorter than its diff:
```python
import functools

import jax
import jax.numpy as jnp
from jax import lax
from jax.experimental import pallas as pl
from jax.experimental.pallas import tpu as pltpu
from jax.sharding import PartitionSpec as P

MESH = pl.DeviceIdType.MESH
f32, bf16, i32 = jnp.float32, jnp.bfloat16, jnp.int32
LANES = 128
CHUNK = 256
FINE_SIDES = ((-1, -1), (-1, 0), (-1, 1), (0, -1), (0, 1), (1, -1), (1, 0), (1, 1))
COARSE_SIDES = (-2, -1, 1, 2)
EDGE_OWN, EDGE_FROM, EDGE_TO, EDGE_OUT, NODE_OWN, NODE_SUM, NODE_OUT = range(7)


def halves(values):
    high = values.astype(bf16)
    return high, (values - high.astype(f32)).astype(bf16)


def wide_halves(values):
    return jnp.concatenate(halves(values), axis=1)


def fold(product):
    return product[:, :LANES] + product[:, LANES:]


def dot(left, right):
    return jnp.dot(left, right, preferred_element_type=f32)


def mm(values, weight):
    return fold(dot(wide_halves(values), weight))


def normed(centered):
    return centered * lax.rsqrt(jnp.mean(centered * centered, axis=-1, keepdims=True) + 1e-05)


def as_columns(row):
    return jnp.broadcast_to(row, (LANES, LANES)).T


def lookup(levels, table):
    found = jnp.zeros(levels.shape, f32)
    for level in range(table.shape[0]):
        found = jnp.where(levels == level, table[level], found)
    return found


def sub_iota(shape):
    return lax.broadcasted_iota(i32, shape, 0)


def lane_iota(shape):
    return lax.broadcasted_iota(i32, shape, 1)


def span(start, size):
    return pl.ds(pl.multiple_of(start, size), size)


def take_rows(index, start, count, table, out):
    window = index.shape[0] - CHUNK + 1

    def some(b, carry):
        first = pl.multiple_of(b * CHUNK, CHUNK)
        there = out.at[pl.ds(first, CHUNK)]
        for j in range(CHUNK):
            place = index.at[pl.ds(j, window)][start + first]
            there[pl.ds(j, 1), :] = table[pl.ds(place, 1), :]
        return carry

    lax.fori_loop(0, count // CHUNK, some, 0)


def take_lists(lists, table, out):
    count, length = out.shape[0], out.shape[1]

    def one(k, carry):
        there = out.at[k]
        for j in range(length):
            there[pl.ds(j, 1), :] = table[pl.ds(lists[0, k, j], 1), :]
        return carry

    lax.fori_loop(0, count, one, 0)


def place_of():
    return lax.axis_index("wide"), lax.axis_index("narrow")


def remote_copy(src, dst, send_sem, recv_sem, where):
    return pltpu.make_async_remote_copy(
        src_ref=src, dst_ref=dst, send_sem=send_sem, recv_sem=recv_sem,
        device_id=where, device_id_type=MESH,
    )


def greetings():
    barrier = pltpu.get_barrier_semaphore()

    def signal(where):
        pl.semaphore_signal(barrier, inc=1, device_id=where, device_id_type=MESH)

    return signal, lambda count: pl.semaphore_wait(barrier, count)


def kernel(
    sizes,
    sender, send, csender, csend, rsource, rtile, rtable, ptable,
    foff, coff, crow, roff, rlevel, pindex, plevel,
    x_in, e_in, ce_in, ew1, ew2, nw1, nw2,
    out, cout,
    x, e, base, table, xc, xv, agg, ga, gb, ohg, ohs, wd,
    r_ew1, r_ew2, r_nw1, r_nw2,
    hout1, hin1, hout2, hin2,
    scale, roh, rsel, picked, contrib, rs_out, rs_in, dd_out, dd_in,
    cx, ce, cbase, ctable, cohg, cohs, cohh, cpick, chout1, chout2, chin1, chin2, cxc, cxv, cagg, cfull,
    amat,
    local_sem, h1s, h1r, h2s, h2r, rss, rsr, dds, ddr, ags, agr,
    c1s, c1r, c2s, c2r,
):
    W, N = sizes
    w, n = place_of()
    nodes, slots = x.shape[0], e.shape[0]
    halo = send.shape[2]
    tiles = nodes // LANES
    per_tile = slots // tiles
    unit = 4 * per_tile
    cown = cfull.shape[0]
    chalo = csend.shape[2]
    cslots = ce.shape[0]
    blocks = rsource.shape[0] // LANES

    def inside(dw, dn):
        return (w + dw >= 0) & (w + dw < W) & (n + dn >= 0) & (n + dn < N)

    def remote(src, dst, send_sem, recv_sem, where):
        return remote_copy(src, dst, send_sem, recv_sem, where)

    def peer(d):
        return lax.rem(n + d, N)

    loads = [
        pltpu.make_async_copy(x_in, x, local_sem.at[0]),
        pltpu.make_async_copy(ew1, r_ew1, local_sem.at[1]),
        pltpu.make_async_copy(ew2, r_ew2, local_sem.at[2]),
        pltpu.make_async_copy(nw1, r_nw1, local_sem.at[3]),
        pltpu.make_async_copy(nw2, r_nw2, local_sem.at[4]),
        pltpu.make_async_copy(e_in, e, local_sem.at[5]),
        pltpu.make_async_copy(ce_in, ce, local_sem.at[6]),
    ]
    for load in loads:
        load.start()

    signal, wait_for = greetings()
    others = [(dw, dn) for dw, dn in FINE_SIDES if dw] + [(-2, 0), (2, 0)]
    for d in range(1, N):
        signal((w, peer(d)))
    expected = i32(N - 1)
    for dw, dn in others:
        @pl.when(inside(dw, dn))
        def _():
            signal((w + dw, n + dn))
        expected = expected + inside(dw, dn).astype(i32)

    def fine_copy(k, hout, hin, ss, rs, where):
        return remote(hout.at[k], hin.at[k], ss.at[k], rs.at[k], where)

    def fine_start(k, hout, hin, ss, rs):
        dw, dn = FINE_SIDES[k]

        @pl.when(inside(dw, dn))
        def _():
            fine_copy(k, hout, hin, ss, rs, (w + dw, n + dn)).start()

    def fine_arrive(k, hout, hin, ss, rs):
        dw, dn = FINE_SIDES[k]

        @pl.when(inside(-dw, -dn))
        def _():
            fine_copy(k, hout, hin, ss, rs, (w - dw, n - dn)).wait_recv()

        @pl.when(jnp.logical_not(inside(-dw, -dn)))
        def _():
            hin[k] = jnp.zeros(hin.shape[1:], f32)

    def fine_sent(k, hout, hin, ss, rs):
        dw, dn = FINE_SIDES[k]

        @pl.when(inside(dw, dn))
        def _():
            fine_copy(k, hout, hin, ss, rs, (w + dw, n + dn)).wait_send()

    loads[0].wait()
    take_lists(send, x, hout1)
    wait_for(expected)
    for k in range(8):
        fine_start(k, hout1, hin1, h1s, h1r)

    for load in loads[1:5]:
        load.wait()

    def put_weight(section, place, value):
        high, low = halves(value)
        wide = jnp.concatenate([high, low], axis=1)
        wd[section * 7 + place] = jnp.concatenate([wide, wide], axis=0)

    def center(value):
        return value - jnp.mean(value, axis=1, keepdims=True)

    def prepare(s):
        put_weight(s, EDGE_OWN, r_ew1[s, 0:128, :])
        put_weight(s, EDGE_FROM, r_ew1[s, 128:256, :])
        put_weight(s, EDGE_TO, r_ew1[s, 256:384, :])
        put_weight(s, EDGE_OUT, center(r_ew2[s]))
        put_weight(s, NODE_OWN, r_nw1[s, 0:128, :])
        put_weight(s, NODE_SUM, r_nw1[s, 128:256, :])
        put_weight(s, NODE_OUT, center(r_nw2[s]))

    prepare(0)

    def weight(s, place):
        return wd[s * 7 + place]

    lanes = lane_iota((LANES, LANES))
    rows = sub_iota((LANES, LANES))
    per_block = per_tile // LANES

    def one_hots(t, carry):
        for c in range(per_block):
            row = foff[pl.ds(t * per_block + c, 1), :]
            to = as_columns(jnp.minimum(row, LANES - 1))
            ohg[span(t * per_tile + c * LANES, LANES), :] = (to == lanes).astype(f32).astype(bf16)
            ohs[span(t * LANES, LANES), c * LANES : (c + 1) * LANES] = (
                (rows == row).astype(f32).astype(bf16)
            )
        return carry

    lax.fori_loop(0, tiles, one_hots, 0, unroll=4)

    def fine_own(s):
        for b in range(nodes // 1024):
            part = slice(b * 1024, (b + 1) * 1024)
            wide = wide_halves(x[part, :])
            table[part, :] = fold(dot(wide, weight(s, EDGE_FROM)))
            xc[part, :] = wide_halves(fold(dot(wide, weight(s, EDGE_TO))))
            xv[part, :] = fold(dot(wide, weight(s, NODE_OWN)))

    def fine_base_edges(s):
        def one(i, carry):
            part = span(i * unit, unit)
            base[part, :] = mm(e[part, :], weight(s, EDGE_OWN))
            return carry

        lax.fori_loop(0, slots // unit, one, 0)

    def fine_base(s, with_edges):
        def one(i, carry):
            part = span(i * unit, unit)
            own = mm(e[part, :], weight(s, EDGE_OWN)) if with_edges else base[part, :]
            to = []
            for t in range(unit // per_tile):
                here = ohg[span(i * unit + t * per_tile, per_tile), :]
                there = xc[span(i * (unit // 4) + t * LANES, LANES), :]
                to.append(fold(dot(here, there)))
            base[part, :] = own + jnp.concatenate(to, axis=0)
            return carry

        lax.fori_loop(0, slots // unit, one, 0)

    def fine_halo_in(s, hout, hin, ss, rs):
        for k in range(8):
            fine_arrive(k, hout, hin, ss, rs)
        rows_in = jnp.concatenate([hin[k] for k in range(8)], axis=0)
        table[nodes:, :] = mm(rows_in, weight(s, EDGE_FROM))

    def fine_edges_nodes(s, keep, write):
        def some(i, carry):
            part = span(i * unit, unit)
            take_rows(sender, i * unit, unit, table, ga)
            h = jnp.maximum(base[part, :] + ga[...], 0.0)
            fresh = e[part, :] + normed(mm(h, weight(s, EDGE_OUT)))
            if keep:
                e[part, :] = fresh
            wide = wide_halves(fresh)
            for t in range(unit // per_tile):
                q = span(i * (unit // 4) + t * LANES, LANES)
                agg[q, :] = fold(dot(ohs[q, :], wide[t * per_tile : (t + 1) * per_tile]))
            return carry

        lax.fori_loop(0, slots // unit, some, 0)
        for b in range(nodes // 1024):
            part = slice(b * 1024, (b + 1) * 1024)
            h = jnp.maximum(xv[part, :] + mm(agg[part, :], weight(s, NODE_SUM)), 0.0)
            write(part, x[part, :] + normed(mm(h, weight(s, NODE_OUT))))

    fine_own(0)
    loads[5].wait()
    fine_base(0, True)
    fine_halo_in(0, hout1, hin1, h1s, h1r)

    def keep_nodes(part, value):
        x[part, :] = value

    fine_edges_nodes(0, True, keep_nodes)

    scale[...] = lookup(rlevel[...], rtable)

    take_rows(rsource, 0, blocks * LANES, x, picked)

    def restrict_block(b, carry):
        row = roff[pl.ds(b, 1), :]
        hit = rows == row
        roh[:, span(b * LANES, LANES)] = hit.astype(f32).astype(bf16)
        left = wide_halves(jnp.where(hit, scale[pl.ds(b, 1), :], 0.0))
        right = wide_halves(picked[span(b * LANES, LANES), :])
        contrib[b] = fold(dot(left, jnp.concatenate([right, right], axis=0)))
        return carry

    lax.fori_loop(0, blocks, restrict_block, 0, unroll=8)

    def restrict_tile(t):
        def add(b, total):
            return total + contrib[b] * (rtile[b] == t).astype(f32)

        rs_out[t] = lax.fori_loop(0, blocks, add, jnp.zeros((LANES, LANES), f32), unroll=8)

    core, chip = lax.rem(n, 2), lax.div(n, 2)
    pair = n + 1 - 2 * core
    chips = N // 2

    def pair_copy(i, tile):
        return remote(rs_out.at[tile], rs_in.at[i], rss.at[i], rsr.at[i], (w, pair))

    def cross_copy(d, tile, toward):
        slot = chips + d
        return remote(rs_out.at[tile], rs_in.at[slot], rss.at[slot], rsr.at[slot], (w, toward))

    for i in range(chips):
        restrict_tile(2 * i + 1 - core)
        pair_copy(i, 2 * i + 1 - core).start()

    def select_block(b, carry):
        kept = jnp.where(sub_iota((8, LANES)) == rtile[b], scale[pl.ds(b, 1), :], 0.0)
        high = kept.astype(bf16).astype(f32)
        rsel[:, span(b * LANES, LANES)] = jnp.concatenate([high, kept - high], axis=0).astype(bf16)
        return carry

    lax.fori_loop(0, blocks, select_block, 0, unroll=8)
    weights = lax.dot_general(
        rsel[...], roh[...], (((1,), (1,)), ((), ())), preferred_element_type=f32
    )
    weights = weights[0:8] + weights[8:16]
    for t in range(N):
        dd_out[t] = jnp.broadcast_to(weights[t : t + 1], (8, LANES))

    def weight_copy(d, toward):
        return remote(dd_out.at[peer(d)], dd_in.at[d], dds.at[d], ddr.at[d], (w, toward))

    for d in range(1, N):
        weight_copy(d, peer(d)).start()
    for i in range(chips):
        restrict_tile(2 * i + core)
    for d in (2, 1, 3, 0):
        place = lax.rem(chip + d, chips)
        tile = 2 * place + core
        pair_copy(place, tile).wait_recv()
        rs_out[tile] = rs_out[tile] + rs_in[place]
        if d:
            cross_copy(d, tile, peer(2 * d)).start()

    cper_tile = cslots // (cown // LANES)

    def coarse_base_edges(s):
        for i in range(cslots // unit):
            part = slice(i * unit, (i + 1) * unit)
            cbase[part, :] = mm(ce[part, :], weight(s, EDGE_OWN))

    prepare(1)

    def prolong_block(b, carry):
        part = span(b * LANES, LANES)
        raw = [lookup(plevel[k : k + 1, part], ptable) for k in range(3)]
        total = raw[0] + raw[1] + raw[2]
        places = [as_columns(pindex[k : k + 1, part]) for k in range(3)]
        amounts = [as_columns(r / total) for r in raw]
        for c in range(cown // LANES):
            value = jnp.zeros((LANES, LANES), f32)
            for k in range(3):
                value = value + jnp.where(places[k] == lanes + c * LANES, amounts[k], 0.0)
            high, low = halves(value)
            amat[part, c * LANES : (c + 1) * LANES] = high
            amat[part, cown + c * LANES : cown + (c + 1) * LANES] = low
        return carry

    def prolong_weights(part):
        lax.fori_loop(part * tiles // 4, (part + 1) * tiles // 4, prolong_block, 0, unroll=2)

    def coarse_one_hots(t, carry):
        for c in range(cper_tile // LANES):
            block = t * (cper_tile // LANES) + c
            row = coff[pl.ds(block, 1), :]
            part = span(block * LANES, LANES)
            cohg[part, :] = (as_columns(jnp.minimum(row, LANES - 1)) == lanes).astype(f32).astype(bf16)
            cohs[span(t * LANES, LANES), c * LANES : (c + 1) * LANES] = (
                (rows == row).astype(f32).astype(bf16)
            )
            origin = as_columns(crow[pl.ds(block, 1), :]) - cown
            for h in range(4 * chalo // LANES):
                cohh[part, h * LANES : (h + 1) * LANES] = (
                    (origin == lanes + h * LANES).astype(f32).astype(bf16)
                )
        return carry

    lax.fori_loop(0, cown // LANES, coarse_one_hots, 0, unroll=2)
    ctable[cown:, :] = jnp.zeros((4 * chalo, LANES), f32)
    loads[6].wait()
    prolong_weights(0)
    prolong_weights(1)

    own = span(n * LANES, LANES)
    numer = rs_out[n]
    for d in range(1, chips):
        cross_copy(d, n, peer(N - 2 * d)).wait_recv()
        numer = numer + rs_in[chips + d]
    denom = dd_out[n]
    for d in range(1, N):
        weight_copy(d, peer(N - d)).wait_recv()
        denom = denom + dd_in[d]
    cx[own, :] = numer / (1.0 + as_columns(denom[0:1]))

    def gather_copy(slot, tile, toward):
        place = cx.at[span(tile * LANES, LANES)]
        return remote(place, place, ags.at[slot], agr.at[slot], (w, toward))

    for d in (2, 1, 3):
        gather_copy(d, n, peer(2 * d)).start()
    gather_copy(0, n, pair).start()
    prepare(2)
    prepare(3)
    prolong_weights(2)
    fine_base_edges(3)
    coarse_base_edges(1)
    for d in (1, 3, 2):
        tile = peer(N - 2 * d)
        gather_copy(d, tile, tile).wait_recv()
        gather_copy(chips + d, tile, pair).start()
    prolong_weights(3)
    gather_copy(0, pair, pair).wait_recv()
    for d in (1, 3, 2):
        gather_copy(chips + d, lax.rem(pair + N - 2 * d, N), pair).wait_recv()

    def coarse_copy(k, chin, chout, ss, rs, toward):
        return remote(chout.at[k], chin.at[k], ss.at[k], rs.at[k], (toward, n))

    def coarse_step(s, chin, chout, cs, cr, keep):
        take_lists(csend, cx, cpick)
        for k in range(4):
            chout[k] = mm(cpick[k], weight(s, EDGE_FROM))
        for k, dw in enumerate(COARSE_SIDES):
            @pl.when(inside(dw, 0))
            def _():
                coarse_copy(k, chin, chout, cs, cr, w + dw).start()

        wide = wide_halves(cx[...])
        ctable[0:cown, :] = fold(dot(wide, weight(s, EDGE_FROM)))
        cxc[...] = wide_halves(fold(dot(wide, weight(s, EDGE_TO))))
        cxv[...] = fold(dot(wide, weight(s, NODE_OWN)))
        if s != 1:
            coarse_base_edges(s)
        for i, buffer in enumerate((ga, gb)):
            part = slice(i * unit, (i + 1) * unit)
            take_rows(csender, i * unit, unit, ctable, buffer)
            to = []
            for t in range(unit // cper_tile):
                q = i * unit + t * cper_tile
                tile = i * (unit // cper_tile) + t
                here = cohg[q : q + cper_tile, :]
                to.append(fold(dot(here, cxc[tile * LANES : (tile + 1) * LANES, :])))
            buffer[...] = buffer[...] + (cbase[part, :] + jnp.concatenate(to, axis=0))
        for k, dw in enumerate(COARSE_SIDES):
            @pl.when(inside(-dw, 0))
            def _():
                coarse_copy(k, chin, chout, cs, cr, w - dw).wait_recv()

            @pl.when(jnp.logical_not(inside(-dw, 0)))
            def _():
                chin[k] = jnp.zeros((chalo, LANES), f32)

        far = wide_halves(jnp.concatenate([chin[k] for k in range(4)], axis=0))
        for i, buffer in enumerate((ga, gb)):
            part = slice(i * unit, (i + 1) * unit)
            h = jnp.maximum(buffer[...] + fold(dot(cohh[part, :], far)), 0.0)
            fresh = ce[part, :] + normed(mm(h, weight(s, EDGE_OUT)))
            if keep:
                ce[part, :] = fresh
            wide = wide_halves(fresh)
            for t in range(unit // cper_tile):
                q = (i * (unit // cper_tile) + t) * LANES
                cagg[q : q + LANES, :] = fold(
                    dot(cohs[q : q + LANES, :], wide[t * cper_tile : (t + 1) * cper_tile])
                )
        h = jnp.maximum(cxv[...] + mm(cagg[...], weight(s, NODE_SUM)), 0.0)
        fresh = cx[...] + normed(mm(h, weight(s, NODE_OUT)))
        if keep:
            for d in (2, 1, 3):
                gather_copy(d, n, peer(2 * d)).wait_send()
                gather_copy(chips + d, peer(N - 2 * d), pair).wait_send()
            gather_copy(0, n, pair).wait_send()
            cx[...] = fresh
        else:
            cfull[...] = fresh

    coarse_step(1, chin1, chout1, c1s, c1r, True)
    coarse_step(2, chin2, chout2, c2s, c2r, False)

    cstore = pltpu.make_async_copy(cfull, cout, local_sem.at[7])
    cstore.start()
    cwide = wide_halves(cfull[...])
    for b in range(nodes // 1024):
        part = slice(b * 1024, (b + 1) * 1024)
        total = dot(amat[part, 0:cown], cwide) + dot(amat[part, cown:], cwide)
        x[part, :] = x[part, :] + fold(total)

    take_lists(send, x, hout2)
    for k in range(8):
        fine_start(k, hout2, hin2, h2s, h2r)
    fine_own(3)
    fine_base(3, False)
    fine_halo_in(3, hout2, hin2, h2s, h2r)

    def write_nodes(part, value):
        agg[part, :] = value

    fine_edges_nodes(3, False, write_nodes)
    store = pltpu.make_async_copy(agg, out, local_sem.at[0])
    store.start()

    for k in range(8):
        fine_sent(k, hout1, hin1, h1s, h1r)
        fine_sent(k, hout2, hin2, h2s, h2r)
    for d in range(1, N):
        weight_copy(d, peer(d)).wait_send()
    for i in range(chips):
        pair_copy(i, 2 * i + 1 - core).wait_send()
    for d in (2, 1, 3):
        cross_copy(d, 2 * lax.rem(chip + d, chips) + core, peer(2 * d)).wait_send()
    for k, dw in enumerate(COARSE_SIDES):
        @pl.when(inside(dw, 0))
        def _():
            coarse_copy(k, chin1, chout1, c1s, c1r, w + dw).wait_send()
            coarse_copy(k, chin2, chout2, c2s, c2r, w + dw).wait_send()
    cstore.wait()
    store.wait()


def local(
    W, N,
    fine_nodes, fine_edges, fine_sender, fine_offset, fine_send,
    coarse_edges, coarse_sender, coarse_offset, coarse_send,
    restrict_source, restrict_offset, restrict_tile, restrict_weight,
    prolong_index, prolong_weight, restrict_table, prolong_table,
    edge_w1, edge_w2, node_w1, node_w2,
):
    nodes, slots = fine_nodes.shape[0], fine_edges.shape[0]
    halo, chalo = fine_send.shape[2], coarse_send.shape[2]
    tiles = nodes // LANES
    per_tile = slots // tiles
    cown = N * LANES
    cslots = coarse_edges.shape[0]
    blocks = restrict_tile.shape[0]
    smem = pl.BlockSpec(memory_space=pltpu.SMEM)
    vmem = pl.BlockSpec(memory_space=pltpu.VMEM)
    hbm = pl.BlockSpec(memory_space=pl.ANY)

    def F(*shape):
        return pltpu.VMEM(shape, f32)

    def B(*shape):
        return pltpu.VMEM(shape, bf16)

    def D(count):
        return pltpu.SemaphoreType.DMA((count,))

    row = lambda flat: flat.reshape(-1, LANES)
    return pl.pallas_call(
        functools.partial(kernel, (W, N)),
        out_shape=(
            jax.ShapeDtypeStruct((nodes, LANES), f32),
            jax.ShapeDtypeStruct((cown, LANES), f32),
        ),
        in_specs=[smem] * 8 + [vmem] * 7 + [hbm] * 7,
        out_specs=(hbm, hbm),
        scratch_shapes=[
            F(nodes, LANES), F(slots, LANES), F(slots, LANES), F(nodes + 8 * halo, LANES),
            B(nodes, 2 * LANES), F(nodes, LANES), F(nodes, LANES),
            F(4 * per_tile, LANES), F(4 * per_tile, LANES),
            B(slots, LANES), B(nodes, per_tile), B(28, 2 * LANES, 2 * LANES),
            F(*edge_w1.shape), F(*edge_w2.shape), F(*node_w1.shape), F(*node_w2.shape),
            F(8, halo, LANES), F(8, halo, LANES), F(8, halo, LANES), F(8, halo, LANES),
            F(blocks, LANES), B(LANES, blocks * LANES), B(16, blocks * LANES), F(blocks * LANES, LANES),
            F(blocks, LANES, LANES), F(N, LANES, LANES), F(N, LANES, LANES),
            F(N, 8, LANES), F(N, 8, LANES),
            F(cown, LANES), F(cslots, LANES), F(cslots, LANES), F(cown + 4 * chalo, LANES),
            B(cslots, LANES), B(cown, cslots // (cown // LANES)), B(cslots, 4 * chalo),
            F(4, chalo, LANES), F(4, chalo, LANES), F(4, chalo, LANES), F(4, chalo, LANES), F(4, chalo, LANES),
            B(cown, 2 * LANES), F(cown, LANES), F(cown, LANES), F(cown, LANES),
            B(nodes, 2 * cown),
            D(8), D(8), D(8), D(8), D(8), D(N), D(N), D(N), D(N),
            D(N), D(N), D(4), D(4), D(4), D(4),
        ],
        compiler_params=pltpu.CompilerParams(
            collective_id=0, has_side_effects=True, vmem_limit_bytes=60 << 20
        ),
        name="graph_window",
    )(
        fine_sender, fine_send, coarse_sender, coarse_send, restrict_source, restrict_tile,
        restrict_table, prolong_table,
        row(fine_offset), row(coarse_offset), row(coarse_sender), row(restrict_offset), row(restrict_weight),
        prolong_index, prolong_weight,
        fine_nodes, fine_edges, coarse_edges, edge_w1, edge_w2, node_w1, node_w2,
    )


def solution(mesh):
    both = ("wide", "narrow")
    placed = (
        P(both, None), P(both, None), P(both), P(both), P(both, None, None),
        P("wide", None), P("wide"), P("wide"), P("wide", None, None),
        P(both), P(both), P(both), P(both), P(None, both), P(None, both),
        P(), P(), P(), P(), P(), P(),
    )
    return jax.shard_map(
        functools.partial(local, mesh.shape["wide"], mesh.shape["narrow"]),
        mesh=mesh,
        in_specs=placed,
        out_specs=(P(both, None), P("wide", None)),
        check_vma=False,
    )
```

time: 155 us -> 81 us (0.52); the launches traced: 152 us -> 80.6 us
  Pallas kernels: 147 us -> 75.8 us
    pallas_call x1, Pallas kernels: 147 us -> 75.8 us  [local(): pl.pallas_call(functools.partial(kernel, (W, N)), out_shape=(jax.ShapeDty...]
where the time goes in v2:
time: 81 us; the launch traced here: 80.6 us
  Pallas kernels  75.8 us (94%)
  local copies, waits for them, and re-layouts  4.13 us (5%)
    pallas_call x1, Pallas kernels, local(): pl.pallas_call(functools.partial(kernel, (W, N)), out_shape=(jax.ShapeDty...  75.8 us
    unnamed x2, local copies, waits for them, and re-layouts  4.13 us

profile of v2, /device:TPU:14, one launch (start us, length us, event | category | flops | bytes accessed | tf_op | source)
XLA Modules:
  0.0 80.6 jit_solution(6110987051306802316)
XLA Ops:
  0.6 75.8 %graph_window.1 = (f32[2048,128]{1,0:T(8,128)}, f32[1024,128]{1,0:T(8,128)}) custom-call(s32[8192]{0:T(1024)} %sender.1, s32[1,8,96]{2,1,0:T(8,128)} %send.1, s32[4096]{0:T(1024)} %csender.1, s32[1,4,64]{2,1,0:T(4,128)} %csend.1, s32[5120]{0:T(1024)} %rsource.1, s32[40]{0:T(128)} %rtile.1, f32[16]{0:T(128)} %rtable.1, f32[16]{0:T(128)} %ptable.1, ...), custom_call_target="tpu_custom_call" | custom-call | tf_op jit(solution)/shard_map/graph_window/pallas_call | solution.py:592
  76.5 2.3 %copy.25 = f32[2048,128]{1,0:T(8,128)} copy(f32[2048,128]{1,0:T(8,128)} %get-tuple-element.4) | data formatting | bytes 2097152
  78.7 1.9 %copy.26 = f32[1024,128]{1,0:T(8,128)} copy(f32[1024,128]{1,0:T(8,128)} %get-tuple-element.5) | data formatting | bytes 1048576

commit v3 on v2

--- a/solution.py
+++ b/solution.py
@@ -115,8 +115,8 @@
     sender, send, csender, csend, rsource, rtile, rtable, ptable,
     foff, coff, crow, roff, rlevel, pindex, plevel,
     x_in, e_in, ce_in, ew1, ew2, nw1, nw2,
-    out, cout,
-    x, e, base, table, xc, xv, agg, ga, gb, ohg, ohs, wd,
+    xout, xvout, aggout, wout, cout,
+    x, e, base, table, xc, xv, agg, ga, ohg, ohs, wd,
     r_ew1, r_ew2, r_nw1, r_nw2,
     hout1, hin1, hout2, hin2,
     scale, roh, rsel, picked, contrib, rs_out, rs_in, dd_out, dd_in,
@@ -131,7 +131,7 @@
     halo = send.shape[2]
     tiles = nodes // LANES
     per_tile = slots // tiles
-    unit = 4 * per_tile
+    unit = 8 * per_tile
     cown = cfull.shape[0]
     chalo = csend.shape[2]
     cslots = ce.shape[0]
@@ -155,8 +155,7 @@
         pltpu.make_async_copy(e_in, e, local_sem.at[5]),
         pltpu.make_async_copy(ce_in, ce, local_sem.at[6]),
     ]
-    for load in loads:
-        load.start()
+    loads[0].start()
 
     signal, wait_for = greetings()
     others = [(dw, dn) for dw, dn in FINE_SIDES if dw] + [(-2, 0), (2, 0)]
@@ -172,12 +171,21 @@
     def fine_copy(k, hout, hin, ss, rs, where):
         return remote(hout.at[k], hin.at[k], ss.at[k], rs.at[k], where)
 
-    def fine_start(k, hout, hin, ss, rs):
-        dw, dn = FINE_SIDES[k]
-
-        @pl.when(inside(dw, dn))
-        def _():
-            fine_copy(k, hout, hin, ss, rs, (w + dw, n + dn)).start()
+    def send_halo(hout, hin, ss, rs):
+        def one(k, carry):
+            there = hout.at[k]
+            for j in range(halo):
+                there[pl.ds(j, 1), :] = x[pl.ds(send[0, k, j], 1), :]
+            square = jnp.where(k >= 4, k + 1, k)
+            dw, dn = lax.div(square, 3) - 1, lax.rem(square, 3) - 1
+
+            @pl.when(inside(dw, dn))
+            def _():
+                fine_copy(k, hout, hin, ss, rs, (w + dw, n + dn)).start()
+
+            return carry
+
+        lax.fori_loop(0, 8, one, 0)
 
     def fine_arrive(k, hout, hin, ss, rs):
         dw, dn = FINE_SIDES[k]
@@ -198,10 +206,10 @@
             fine_copy(k, hout, hin, ss, rs, (w + dw, n + dn)).wait_send()
 
     loads[0].wait()
-    take_lists(send, x, hout1)
+    for load in loads[1:]:
+        load.start()
     wait_for(expected)
-    for k in range(8):
-        fine_start(k, hout1, hin1, h1s, h1r)
+    send_halo(hout1, hin1, h1s, h1r)
 
     for load in loads[1:5]:
         load.wait()
@@ -267,7 +275,7 @@
             to = []
             for t in range(unit // per_tile):
                 here = ohg[span(i * unit + t * per_tile, per_tile), :]
-                there = xc[span(i * (unit // 4) + t * LANES, LANES), :]
+                there = xc[span((i * (unit // per_tile) + t) * LANES, LANES), :]
                 to.append(fold(dot(here, there)))
             base[part, :] = own + jnp.concatenate(to, axis=0)
             return carry
@@ -280,35 +288,30 @@
         rows_in = jnp.concatenate([hin[k] for k in range(8)], axis=0)
         table[nodes:, :] = mm(rows_in, weight(s, EDGE_FROM))
 
-    def fine_edges_nodes(s, keep, write):
-        def some(i, carry):
-            part = span(i * unit, unit)
-            take_rows(sender, i * unit, unit, table, ga)
-            h = jnp.maximum(base[part, :] + ga[...], 0.0)
-            fresh = e[part, :] + normed(mm(h, weight(s, EDGE_OUT)))
-            if keep:
-                e[part, :] = fresh
-            wide = wide_halves(fresh)
-            for t in range(unit // per_tile):
-                q = span(i * (unit // 4) + t * LANES, LANES)
-                agg[q, :] = fold(dot(ohs[q, :], wide[t * per_tile : (t + 1) * per_tile]))
-            return carry
-
-        lax.fori_loop(0, slots // unit, some, 0)
+    def fine_edges_sums(s, keep):
+        take_rows(sender, 0, slots, table, ga)
+        h = jnp.maximum(base[...] + ga[...], 0.0)
+        fresh = e[...] + normed(mm(h, weight(s, EDGE_OUT)))
+        if keep:
+            e[...] = fresh
+        wide = wide_halves(fresh)
+        for t in range(tiles):
+            q = slice(t * LANES, (t + 1) * LANES)
+            agg[q, :] = fold(dot(ohs[q, :], wide[t * per_tile : (t + 1) * per_tile]))
+
+    def fine_nodes_update(s):
         for b in range(nodes // 1024):
             part = slice(b * 1024, (b + 1) * 1024)
             h = jnp.maximum(xv[part, :] + mm(agg[part, :], weight(s, NODE_SUM)), 0.0)
-            write(part, x[part, :] + normed(mm(h, weight(s, NODE_OUT))))
+            x[part, :] = x[part, :] + normed(mm(h, weight(s, NODE_OUT)))
 
     fine_own(0)
     loads[5].wait()
     fine_base(0, True)
     fine_halo_in(0, hout1, hin1, h1s, h1r)
 
-    def keep_nodes(part, value):
-        x[part, :] = value
-
-    fine_edges_nodes(0, True, keep_nodes)
+    fine_edges_sums(0, True)
+    fine_nodes_update(0)
 
     scale[...] = lookup(rlevel[...], rtable)
 
@@ -323,7 +326,7 @@
         contrib[b] = fold(dot(left, jnp.concatenate([right, right], axis=0)))
         return carry
 
-    lax.fori_loop(0, blocks, restrict_block, 0, unroll=8)
+    lax.fori_loop(0, blocks, restrict_block, 0, unroll=20)
 
     def restrict_tile(t):
         def add(b, total):
@@ -378,9 +381,7 @@
     cper_tile = cslots // (cown // LANES)
 
     def coarse_base_edges(s):
-        for i in range(cslots // unit):
-            part = slice(i * unit, (i + 1) * unit)
-            cbase[part, :] = mm(ce[part, :], weight(s, EDGE_OWN))
+        cbase[...] = mm(ce[...], weight(s, EDGE_OWN))
 
     prepare(1)
 
@@ -456,6 +457,8 @@
     for d in (1, 3, 2):
         gather_copy(chips + d, lax.rem(pair + N - 2 * d, N), pair).wait_recv()
 
+    cg = ga.at[pl.ds(0, cslots)]
+
     def coarse_copy(k, chin, chout, ss, rs, toward):
         return remote(chout.at[k], chin.at[k], ss.at[k], rs.at[k], (toward, n))
 
@@ -474,16 +477,12 @@
         cxv[...] = fold(dot(wide, weight(s, NODE_OWN)))
         if s != 1:
             coarse_base_edges(s)
-        for i, buffer in enumerate((ga, gb)):
-            part = slice(i * unit, (i + 1) * unit)
-            take_rows(csender, i * unit, unit, ctable, buffer)
-            to = []
-            for t in range(unit // cper_tile):
-                q = i * unit + t * cper_tile
-                tile = i * (unit // cper_tile) + t
-                here = cohg[q : q + cper_tile, :]
-                to.append(fold(dot(here, cxc[tile * LANES : (tile + 1) * LANES, :])))
-            buffer[...] = buffer[...] + (cbase[part, :] + jnp.concatenate(to, axis=0))
+        take_rows(csender, 0, cslots, ctable, cg)
+        to = []
+        for t in range(cown // LANES):
+            here = cohg[t * cper_tile : (t + 1) * cper_tile, :]
+            to.append(fold(dot(here, cxc[t * LANES : (t + 1) * LANES, :])))
+        cg[...] = cg[...] + (cbase[...] + jnp.concatenate(to, axis=0))
         for k, dw in enumerate(COARSE_SIDES):
             @pl.when(inside(-dw, 0))
             def _():
@@ -494,18 +493,14 @@
                 chin[k] = jnp.zeros((chalo, LANES), f32)
 
         far = wide_halves(jnp.concatenate([chin[k] for k in range(4)], axis=0))
-        for i, buffer in enumerate((ga, gb)):
-            part = slice(i * unit, (i + 1) * unit)
-            h = jnp.maximum(buffer[...] + fold(dot(cohh[part, :], far)), 0.0)
-            fresh = ce[part, :] + normed(mm(h, weight(s, EDGE_OUT)))
-            if keep:
-                ce[part, :] = fresh
-            wide = wide_halves(fresh)
-            for t in range(unit // cper_tile):
-                q = (i * (unit // cper_tile) + t) * LANES
-                cagg[q : q + LANES, :] = fold(
-                    dot(cohs[q : q + LANES, :], wide[t * cper_tile : (t + 1) * cper_tile])
-                )
+        h = jnp.maximum(cg[...] + fold(dot(cohh[...], far)), 0.0)
+        fresh = ce[...] + normed(mm(h, weight(s, EDGE_OUT)))
+        if keep:
+            ce[...] = fresh
+        wide = wide_halves(fresh)
+        for t in range(cown // LANES):
+            q = slice(t * LANES, (t + 1) * LANES)
+            cagg[q, :] = fold(dot(cohs[q, :], wide[t * cper_tile : (t + 1) * cper_tile]))
         h = jnp.maximum(cxv[...] + mm(cagg[...], weight(s, NODE_SUM)), 0.0)
         fresh = cx[...] + normed(mm(h, weight(s, NODE_OUT)))
         if keep:
@@ -528,18 +523,19 @@
         total = dot(amat[part, 0:cown], cwide) + dot(amat[part, cown:], cwide)
         x[part, :] = x[part, :] + fold(total)
 
-    take_lists(send, x, hout2)
-    for k in range(8):
-        fine_start(k, hout2, hin2, h2s, h2r)
+    send_halo(hout2, hin2, h2s, h2r)
+    xstore = pltpu.make_async_copy(x, xout, local_sem.at[0])
+    xstore.start()
     fine_own(3)
+    xvstore = pltpu.make_async_copy(xv, xvout, local_sem.at[1])
+    xvstore.start()
+    wstore = pltpu.make_async_copy(wd.at[pl.ds(3 * 7 + NODE_SUM, 2)], wout, local_sem.at[2])
+    wstore.start()
     fine_base(3, False)
     fine_halo_in(3, hout2, hin2, h2s, h2r)
 
-    def write_nodes(part, value):
-        agg[part, :] = value
-
-    fine_edges_nodes(3, False, write_nodes)
-    store = pltpu.make_async_copy(agg, out, local_sem.at[0])
+    fine_edges_sums(3, False)
+    store = pltpu.make_async_copy(agg, aggout, local_sem.at[3])
     store.start()
 
     for k in range(8):
@@ -557,7 +553,16 @@
             coarse_copy(k, chin1, chout1, c1s, c1r, w + dw).wait_send()
             coarse_copy(k, chin2, chout2, c2s, c2r, w + dw).wait_send()
     cstore.wait()
+    xstore.wait()
+    xvstore.wait()
+    wstore.wait()
     store.wait()
+
+
+def last_nodes(x, xv, agg, weights, coarse, out, coarse_out):
+    h = jnp.maximum(xv[...] + mm(agg[...], weights[0]), 0.0)
+    out[...] = x[...] + normed(mm(h, weights[1]))
+    coarse_out[...] = coarse[...]
 
 
 def local(
@@ -589,18 +594,21 @@
         return pltpu.SemaphoreType.DMA((count,))
 
     row = lambda flat: flat.reshape(-1, LANES)
-    return pl.pallas_call(
+    parts = pl.pallas_call(
         functools.partial(kernel, (W, N)),
         out_shape=(
             jax.ShapeDtypeStruct((nodes, LANES), f32),
+            jax.ShapeDtypeStruct((nodes, LANES), f32),
+            jax.ShapeDtypeStruct((nodes, LANES), f32),
+            jax.ShapeDtypeStruct((2, 2 * LANES, 2 * LANES), bf16),
             jax.ShapeDtypeStruct((cown, LANES), f32),
         ),
         in_specs=[smem] * 8 + [vmem] * 7 + [hbm] * 7,
-        out_specs=(hbm, hbm),
+        out_specs=(hbm,) * 5,
         scratch_shapes=[
             F(nodes, LANES), F(slots, LANES), F(slots, LANES), F(nodes + 8 * halo, LANES),
             B(nodes, 2 * LANES), F(nodes, LANES), F(nodes, LANES),
-            F(4 * per_tile, LANES), F(4 * per_tile, LANES),
+            F(slots, LANES),
             B(slots, LANES), B(nodes, per_tile), B(28, 2 * LANES, 2 * LANES),
             F(*edge_w1.shape), F(*edge_w2.shape), F(*node_w1.shape), F(*node_w2.shape),
             F(8, halo, LANES), F(8, halo, LANES), F(8, halo, LANES), F(8, halo, LANES),
@@ -626,6 +634,21 @@
         prolong_index, prolong_weight,
         fine_nodes, fine_edges, coarse_edges, edge_w1, edge_w2, node_w1, node_w2,
     )
+    steps = 2
+    fine_rows = pl.BlockSpec((nodes // steps, LANES), lambda i: (i, 0))
+    coarse_rows = pl.BlockSpec((cown // steps, LANES), lambda i: (i, 0))
+    return pl.pallas_call(
+        last_nodes,
+        grid=(steps,),
+        out_shape=(
+            jax.ShapeDtypeStruct((nodes, LANES), f32),
+            jax.ShapeDtypeStruct((cown, LANES), f32),
+        ),
+        in_specs=[fine_rows] * 3 + [vmem, coarse_rows],
+        out_specs=(fine_rows, coarse_rows),
+        compiler_params=pltpu.CompilerParams(vmem_limit_bytes=60 << 20),
+        name="last_nodes",
+    )(*parts)
 
 
 def solution(mesh):

time: 81 us -> 78.5 us (0.969)
  local copies, waits for them, and re-layouts: 4.13 us -> 0 us
  Pallas kernels: 75.8 us -> 77.3 us
    unnamed x2 -> x0, local copies, waits for them, and re-layouts: 4.13 us -> none
    pallas_call x0 -> x1, Pallas kernels: none -> 3.97 us  [local(): pl.pallas_call(last_nodes, grid=(steps,), out_shape=(jax.ShapeDtypeStruct...]
    pallas_call x1, Pallas kernels: 75.8 us -> 73.4 us  [local(): pl.pallas_call(functools.partial(kernel, (W, N)), out_shape=(jax.ShapeDty...]
where the time goes in v3:
time: 78.5 us; the launch traced here: 78 us
  Pallas kernels  77.3 us (98%)
    pallas_call x1, Pallas kernels, local(): pl.pallas_call(functools.partial(kernel, (W, N)), out_shape=(jax.ShapeDty...  73.4 us
    pallas_call x1, Pallas kernels, local(): pl.pallas_call(last_nodes, grid=(steps,), out_shape=(jax.ShapeDtypeStruct...  3.97 us

profile of v3, /device:TPU:14, one launch (start us, length us, event | category | flops | bytes accessed | tf_op | source)
XLA Modules:
  0.0 78.0 jit_solution(8424784468641459086)
XLA Ops:
  0.6 73.4 %graph_window.1 = (f32[2048,128]{1,0:T(8,128)}, f32[2048,128]{1,0:T(8,128)}, f32[2048,128]{1,0:T(8,128)}, bf16[2,256,256]{2,1,0:T(8,128)(2,1)}, f32[1024,128]{1,0:T(8,128)}) custom-call(s32[8192]{0:T(1024)} %sender.1, s32[1,8,96]{2,1,0:T(8,128)} %send.1, s32[4096]{0:T(1024)} %csender.1, s32[1,4,64]{2,1,0:T(4,128)} %csend.1, s32[5120]{0:T(1024)} %rsource.1, ...), custom_call_target="tpu_custom_call" | custom-call | tf_op jit(solution)/shard_map/graph_window/pallas_call | solution.py:597
  74.0 4.0 %last_nodes.1 = (f32[2048,128]{1,0:T(8,128)}, f32[1024,128]{1,0:T(8,128)}) custom-call(f32[2048,128]{1,0:T(8,128)} %get-tuple-element.7.x, f32[2048,128]{1,0:T(8,128)} %get-tuple-element.8.xv, f32[2048,128]{1,0:T(8,128)} %get-tuple-element.9.agg, bf16[2,256,256]{2,1,0:T(8,128)(2,1)} %get-tuple-element.10.weights, f32[1024,128]{1,0:T(8,128)} %get-tuple-element.11.coarse), custom_call_target="tpu_custom_call" | custom-call | tf_op jit(solution)/shard_map/last_nodes/pallas_call | solution.py:640

commit v4 on v3

--- a/solution.py
+++ b/solution.py
@@ -38,7 +38,8 @@
 
 
 def normed(centered):
-    return centered * lax.rsqrt(jnp.mean(centered * centered, axis=-1, keepdims=True) + 1e-05)
+    spread = jnp.sum(centered * centered, axis=-1, keepdims=True) * (1.0 / LANES)
+    return centered * lax.rsqrt(spread + 1e-05)
 
 
 def as_columns(row):
@@ -171,10 +172,10 @@
     def fine_copy(k, hout, hin, ss, rs, where):
         return remote(hout.at[k], hin.at[k], ss.at[k], rs.at[k], where)
 
-    def send_halo(hout, hin, ss, rs):
+    def send_halo(hout, hin, ss, rs, pick):
         def one(k, carry):
             there = hout.at[k]
-            for j in range(halo):
+            for j in range(halo if pick else 0):
                 there[pl.ds(j, 1), :] = x[pl.ds(send[0, k, j], 1), :]
             square = jnp.where(k >= 4, k + 1, k)
             dw, dn = lax.div(square, 3) - 1, lax.rem(square, 3) - 1
@@ -208,8 +209,9 @@
     loads[0].wait()
     for load in loads[1:]:
         load.start()
+    take_lists(send, x, hout1)
     wait_for(expected)
-    send_halo(hout1, hin1, h1s, h1r)
+    send_halo(hout1, hin1, h1s, h1r, False)
 
     for load in loads[1:5]:
         load.wait()
@@ -260,18 +262,10 @@
             xc[part, :] = wide_halves(fold(dot(wide, weight(s, EDGE_TO))))
             xv[part, :] = fold(dot(wide, weight(s, NODE_OWN)))
 
-    def fine_base_edges(s):
+    def fine_base(s):
         def one(i, carry):
             part = span(i * unit, unit)
-            base[part, :] = mm(e[part, :], weight(s, EDGE_OWN))
-            return carry
-
-        lax.fori_loop(0, slots // unit, one, 0)
-
-    def fine_base(s, with_edges):
-        def one(i, carry):
-            part = span(i * unit, unit)
-            own = mm(e[part, :], weight(s, EDGE_OWN)) if with_edges else base[part, :]
+            own = mm(e[part, :], weight(s, EDGE_OWN))
             to = []
             for t in range(unit // per_tile):
                 here = ohg[span(i * unit + t * per_tile, per_tile), :]
@@ -307,7 +301,7 @@
 
     fine_own(0)
     loads[5].wait()
-    fine_base(0, True)
+    fine_base(0)
     fine_halo_in(0, hout1, hin1, h1s, h1r)
 
     fine_edges_sums(0, True)
@@ -349,25 +343,6 @@
         restrict_tile(2 * i + 1 - core)
         pair_copy(i, 2 * i + 1 - core).start()
 
-    def select_block(b, carry):
-        kept = jnp.where(sub_iota((8, LANES)) == rtile[b], scale[pl.ds(b, 1), :], 0.0)
-        high = kept.astype(bf16).astype(f32)
-        rsel[:, span(b * LANES, LANES)] = jnp.concatenate([high, kept - high], axis=0).astype(bf16)
-        return carry
-
-    lax.fori_loop(0, blocks, select_block, 0, unroll=8)
-    weights = lax.dot_general(
-        rsel[...], roh[...], (((1,), (1,)), ((), ())), preferred_element_type=f32
-    )
-    weights = weights[0:8] + weights[8:16]
-    for t in range(N):
-        dd_out[t] = jnp.broadcast_to(weights[t : t + 1], (8, LANES))
-
-    def weight_copy(d, toward):
-        return remote(dd_out.at[peer(d)], dd_in.at[d], dds.at[d], ddr.at[d], (w, toward))
-
-    for d in range(1, N):
-        weight_copy(d, peer(d)).start()
     for i in range(chips):
         restrict_tile(2 * i + core)
     for d in (2, 1, 3, 0):
@@ -377,6 +352,26 @@
         rs_out[tile] = rs_out[tile] + rs_in[place]
         if d:
             cross_copy(d, tile, peer(2 * d)).start()
+
+    def select_block(b, carry):
+        kept = jnp.where(sub_iota((8, LANES)) == rtile[b], scale[pl.ds(b, 1), :], 0.0)
+        high = kept.astype(bf16).astype(f32)
+        rsel[:, span(b * LANES, LANES)] = jnp.concatenate([high, kept - high], axis=0).astype(bf16)
+        return carry
+
+    lax.fori_loop(0, blocks, select_block, 0, unroll=8)
+    weights = lax.dot_general(
+        rsel[...], roh[...], (((1,), (1,)), ((), ())), preferred_element_type=f32
+    )
+    weights = weights[0:8] + weights[8:16]
+    for t in range(N):
+        dd_out[t] = jnp.broadcast_to(weights[t : t + 1], (8, LANES))
+
+    def weight_copy(d, toward):
+        return remote(dd_out.at[peer(d)], dd_in.at[d], dds.at[d], ddr.at[d], (w, toward))
+
+    for d in range(1, N):
+        weight_copy(d, peer(d)).start()
 
     cper_tile = cslots // (cown // LANES)
 
@@ -423,7 +418,6 @@
     ctable[cown:, :] = jnp.zeros((4 * chalo, LANES), f32)
     loads[6].wait()
     prolong_weights(0)
-    prolong_weights(1)
 
     own = span(n * LANES, LANES)
     numer = rs_out[n]
@@ -445,8 +439,8 @@
     gather_copy(0, n, pair).start()
     prepare(2)
     prepare(3)
+    prolong_weights(1)
     prolong_weights(2)
-    fine_base_edges(3)
     coarse_base_edges(1)
     for d in (1, 3, 2):
         tile = peer(N - 2 * d)
@@ -523,7 +517,7 @@
         total = dot(amat[part, 0:cown], cwide) + dot(amat[part, cown:], cwide)
         x[part, :] = x[part, :] + fold(total)
 
-    send_halo(hout2, hin2, h2s, h2r)
+    send_halo(hout2, hin2, h2s, h2r, True)
     xstore = pltpu.make_async_copy(x, xout, local_sem.at[0])
     xstore.start()
     fine_own(3)
@@ -531,7 +525,7 @@
     xvstore.start()
     wstore = pltpu.make_async_copy(wd.at[pl.ds(3 * 7 + NODE_SUM, 2)], wout, local_sem.at[2])
     wstore.start()
-    fine_base(3, False)
+    fine_base(3)
     fine_halo_in(3, hout2, hin2, h2s, h2r)
 
     fine_edges_sums(3, False)

time: 78.5 us -> 78.6 us (level)
  no operation moved by 1% of the time
where the time goes in v4:
time: 78.6 us; the launch traced here: 78 us
  Pallas kernels  77.4 us (98%)
    pallas_call x1, Pallas kernels, local(): pl.pallas_call(functools.partial(kernel, (W, N)), out_shape=(jax.ShapeDty...  73.4 us
    pallas_call x1, Pallas kernels, local(): pl.pallas_call(last_nodes, grid=(steps,), out_shape=(jax.ShapeDtypeStruct...  3.97 us

profile of v4, /device:TPU:14, one launch (start us, length us, event | category | flops | bytes accessed | tf_op | source)
XLA Modules:
  0.0 78.0 jit_solution(4509134578999604606)
XLA Ops:
  0.6 73.4 %graph_window.1 = (f32[2048,128]{1,0:T(8,128)}, f32[2048,128]{1,0:T(8,128)}, f32[2048,128]{1,0:T(8,128)}, bf16[2,256,256]{2,1,0:T(8,128)(2,1)}, f32[1024,128]{1,0:T(8,128)}) custom-call(s32[8192]{0:T(1024)} %sender.1, s32[1,8,96]{2,1,0:T(8,128)} %send.1, s32[4096]{0:T(1024)} %csender.1, s32[1,4,64]{2,1,0:T(4,128)} %csend.1, s32[5120]{0:T(1024)} %rsource.1, ...), custom_call_target="tpu_custom_call" | custom-call | tf_op jit(solution)/shard_map/graph_window/pallas_call | solution.py:591
  74.1 4.0 %last_nodes.1 = (f32[2048,128]{1,0:T(8,128)}, f32[1024,128]{1,0:T(8,128)}) custom-call(f32[2048,128]{1,0:T(8,128)} %get-tuple-element.7.x, f32[2048,128]{1,0:T(8,128)} %get-tuple-element.8.xv, f32[2048,128]{1,0:T(8,128)} %get-tuple-element.9.agg, bf16[2,256,256]{2,1,0:T(8,128)(2,1)} %get-tuple-element.10.weights, f32[1024,128]{1,0:T(8,128)} %get-tuple-element.11.coarse), custom_call_target="tpu_custom_call" | custom-call | tf_op jit(solution)/shard_map/last_nodes/pallas_call | solution.py:634
